TPU v7x, 32 devices: a whole 2x2x4 slice. The times are simulated.
32 devices in a mesh: stream: 8 (over y, x, core), dp: 4 (over z).
Axes of the slice: x: 2, y: 2, z: 4, core: 2. Of those that a mesh axis runs over, the one named last changes fastest.
Arguments:
- regions: bfloat16 [16384, 768], P(('stream', 'dp')), may hold values from -6 to 6
- cotangent: bfloat16 [16384, 768], P(('stream', 'dp')), may hold values from -6 to 6
- page_lens: int32 [16, 16], replicated, may hold values from 1 to 96, 512 in all within a row
- qkv_weight: float32 [1536, 2304], P('stream'), may hold values from -0.21875 to 0.21875
- out_weight: float32 [1536, 768], P('stream'), may hold values from -1.25 to 1.25
- up_weight: float32 [1536, 3072], P('stream'), may hold values from -0.21875 to 0.21875
- down_weight: float32 [6144, 768], P('stream'), may hold values from -0.109375 to 0.109375
- ln1_gain: float32 [1536], P('stream'), may hold values from 0.5 to 1.5
- ln1_bias: float32 [1536], P('stream'), may hold values from -3 to 3
- ln2_gain: float32 [1536], P('stream'), may hold values from 0.5 to 1.5
- ln2_bias: float32 [1536], P('stream'), may hold values from -3 to 3
- up_bias: float32 [6144], P('stream'), may hold values from -3 to 3
- down_bias: float32 [1536], P('stream'), may hold values from -3 to 3
- gate_own: float32 [1536], P('stream'), may hold values from -0.21875 to 0.21875
- gate_other: float32 [1536], P('stream'), may hold values from -0.21875 to 0.21875
Outputs:
- mixed_rows: bfloat16 [16384, 768], P(('stream', 'dp'))
- region_grad: float32 [16384, 768], P(('stream', 'dp'))
- qkv_weight_grad: float32 [1536, 2304], P('stream')
- out_weight_grad: float32 [1536, 768], P('stream')
- up_weight_grad: float32 [1536, 3072], P('stream')
- down_weight_grad: float32 [6144, 768], P('stream')
- ln1_gain_grad: float32 [1536], P('stream')
- ln1_bias_grad: float32 [1536], P('stream')
- ln2_gain_grad: float32 [1536], P('stream')
- ln2_bias_grad: float32 [1536], P('stream')
- up_bias_grad: float32 [6144], P('stream')
- down_bias_grad: float32 [1536], P('stream')
- gate_own_grad: float32 [1536], P('stream')
- gate_other_grad: float32 [1536], P('stream')
Inputs may be any that keep to these rules, and one draw needn't show every extreme that they name: `page_lens`: each row holds the region counts of the pages packed into one row of 512 regions, in order; a row sums to 512 and its largest count is 96.
All inputs are finite; a program needn't handle non-finite values.
Results may differ from a plain program's by a relative error of at most 0.014.
The roundings to bfloat16 on the way count: a program that leaves them out, or rounds other values in their place, can miss the bound.
Values may be sent and summed in bfloat16 or wider, within the bound.
No kernel may reach another device: no remote copies, remote signals or barrier semaphores. Data moves between devices by JAX's collectives and lax.ppermute only.
A program may use at most 256 MiB of HBM per device.

v0:
```python
import functools
import math

import jax
import jax.numpy as jnp
from jax import lax
from jax.experimental import pallas as pl
from jax.experimental.pallas import tpu as pltpu
from jax.sharding import PartitionSpec as P

D = 768
HEADS = 12
HEAD_DIM = 64
FF = 3072
LEAD = FF - 1280
RUNS = ((LEAD, 768), (LEAD + 768, 512))
SEQ = 512
GROUPS = 2
PART = D // GROUPS
PAIR = 2 * HEAD_DIM
BLOCK = 128
REACH = 96
ROWS = 256
MIB = 1024 * 1024

epsilon = 1e-05
masked_score = -1e30
score_scale = HEAD_DIM ** (-0.5)
gelu_scale = math.sqrt(2.0 / math.pi)
gelu_cubic = 0.044715

f32 = jnp.float32
bf16 = jnp.bfloat16

WINDOWS = [
    (max(0, start - REACH), min(SEQ, start + BLOCK + REACH)) for start in range(0, SEQ, BLOCK)
]
WINDOW = BLOCK + 2 * REACH

in_smem = pl.BlockSpec(memory_space=pltpu.SMEM)
in_vmem = pl.BlockSpec(memory_space=pltpu.VMEM)
in_any = pl.BlockSpec(memory_space=pl.ANY)
in_hbm = pl.BlockSpec(memory_space=pltpu.HBM)


def shape_of(dims, dtype):
    return jax.ShapeDtypeStruct(dims, dtype)


def dot(left, right):
    return lax.dot_general(left, right, (((1,), (0,)), ((), ())), preferred_element_type=f32)


def dot_nt(left, right):
    return lax.dot_general(left, right, (((1,), (1,)), ((), ())), preferred_element_type=f32)


def dot_tn(left, right):
    return lax.dot_general(left, right, (((0,), (0,)), ((), ())), preferred_element_type=f32)


def normalise(values):
    average = jnp.mean(values, axis=-1, keepdims=True)
    centred = values - average
    spread = jnp.mean(centred * centred, axis=-1, keepdims=True)
    root = lax.rsqrt(spread + epsilon)
    return centred * root, root


def norm_back(scaled, root, gain, incoming):
    weighted = incoming * gain
    average = jnp.mean(weighted, axis=-1, keepdims=True)
    slope = jnp.mean(weighted * scaled, axis=-1, keepdims=True)
    return root * (weighted - average - scaled * slope)


def column_sums(values):
    return jnp.sum(values, axis=0, keepdims=True)


class Order:
    def __init__(self):
        self.token = []

    def call(
        self,
        kernel,
        args,
        in_specs,
        outs,
        out_specs,
        scratch=(),
        grid=(),
        limit=16,
        name=None,
        prefetch=None,
        waits=(),
        aliases=None,
        cost=0,
    ):
        given = len(args)
        extra = list(self.token) + list(waits)
        ahead = [] if prefetch is None else [prefetch]
        count = len(ahead)
        smallest = min(math.prod(out.shape) for out in outs)
        marked = smallest > 4096 and not aliases
        outs, out_specs = list(outs), list(out_specs)
        if marked:
            outs.append(shape_of((8, 128), f32))
            out_specs.append(in_vmem)
        place = count + given + len(extra) + len(outs) - 1

        def wrapped(*refs):
            used = list(refs[: count + given]) + list(refs[count + given + len(extra) :])
            if marked:
                refs[place][...] = jnp.zeros((8, 128), f32)
                used.pop(count + given + len(outs) - 1)
            kernel(*used)

        results = pl.pallas_call(
            wrapped,
            out_shape=outs,
            grid_spec=pltpu.PrefetchScalarGridSpec(
                num_scalar_prefetch=count,
                grid=grid,
                in_specs=list(in_specs) + [in_any] * len(extra),
                out_specs=out_specs,
                scratch_shapes=list(scratch),
            ),
            compiler_params=pltpu.CompilerParams(vmem_limit_bytes=limit * MIB),
            cost_estimate=pl.CostEstimate(flops=1 + cost * 10**9, bytes_accessed=1 + cost * MIB, transcendentals=cost * 10**6),
            input_output_aliases=aliases or {},
            name=name,
        )(*ahead, *args, *extra)
        self.token = [min(results, key=lambda out: out.size)]
        return list(results)[:-1] if marked else results

    def hold(self, arrays, waits=()):
        return self.call(
            lambda *refs: None,
            arrays,
            [in_any] * len(arrays),
            [shape_of(array.shape, array.dtype) for array in arrays],
            [in_any] * len(arrays),
            name="hold",
            cost=0,
            waits=waits,
            aliases={k: k for k in range(len(arrays))},
        )

    def pause(self, value):
        return self.call(
            lambda *refs: None,
            [value],
            [in_any],
            [shape_of(value.shape, value.dtype)],
            [in_any],
            name="pause",
            cost=60,
            aliases={0: 0},
        )[0]


def assemble(places, parts, whole):
    rows = whole.shape[0] // len(parts)
    for k, part in enumerate(parts):
        whole[pl.ds(pl.multiple_of(places[k] * rows, 16), rows)] = part[:rows]


def sums_pass(order, places, folds=(), adds=(), pays=(), waits=(), extra=0):
    args, outs, steps = [], [], []

    def give(*arrays):
        args.extend(arrays)
        return list(range(len(args) - len(arrays), len(args)))

    def make(dims, dtype):
        outs.append(shape_of(dims, dtype))
        return len(outs) - 1

    for near, received, widths in folds:
        made = []
        for width in widths:
            rows = near.shape[1] if len(near.shape) == 3 else (near.shape[0] + 16) // 2
            made += [make((rows + add, width), near.dtype) for add in (0, extra)]
        steps.append(("fold", give(near, received), made))
    for left, right in adds:
        steps.append(("add", give(left, right), [make(left.shape, left.dtype)]))
    for mine, received, older, crossed in pays:
        given = give(mine, received, older, crossed)
        steps.append(("pay", given, [make(mine.shape, mine.dtype) for _ in range(2)]))
    count = len(args)

    def kernel(places_ref, *refs):
        ins, results = refs[:count], refs[count:]
        inner = jnp.logical_and(places_ref[4] > 0, places_ref[4] < 3)
        for kind, given, made in steps:
            if kind == "fold" and len(ins[given[0]].shape) == 3:
                first = 0
                for k in range(0, len(made), 2):
                    width = results[made[k]].shape[1]
                    part = slice(first, first + width)
                    for slot in range(2):
                        total = ins[given[0]][slot, :, part].astype(f32)
                        total += ins[given[1]][slot, :, part].astype(f32)
                        results[made[k + slot]][: total.shape[0]] = total.astype(bf16)
                    if extra:
                        results[made[k + 1]][total.shape[0] :] = jnp.zeros((extra, width), bf16)
                    first += width
            elif kind == "fold":
                total = (ins[given[0]][...].astype(f32) + ins[given[1]][...].astype(f32)).astype(bf16)
                rows = results[made[0]].shape[0] - 16
                for slot in range(2):
                    results[made[slot]][:rows] = total[slot * rows : (slot + 1) * rows]
                    results[made[slot]][rows:] = total[2 * rows :]
            elif kind == "add":
                rows = ins[given[0]].shape[0]
                total = ins[given[0]][...].astype(f32) + ins[given[1]][:rows].astype(f32)
                results[made[0]][...] = total.astype(results[made[0]].dtype)
            else:
                rows = ins[given[0]].shape[0]
                fresh = ins[given[0]][...].astype(f32) + ins[given[1]][:rows].astype(f32)
                older = ins[given[2]][...].astype(f32) + ins[given[3]][...].astype(f32)
                results[made[0]][...] = fresh.astype(results[made[0]].dtype)
                results[made[1]][...] = jnp.where(inner, older, fresh).astype(results[made[1]].dtype)

    found = order.call(
        kernel,
        [places, *args],
        [in_smem] + [in_vmem] * len(args),
        outs,
        [in_vmem] * len(outs),
        limit=12,
        name="sums",
        waits=waits,
    )
    found = list(found)
    return found[0] if len(found) == 1 else found


def first_cast_kernel(sizes, qkv, short, out, rows):
    rows[...] = jnp.zeros_like(rows)
    offset = 0
    for line, size in enumerate(sizes):
        rows[line : line + 1, :size] = short[:, offset : offset + size]
        offset += size
    height = qkv.shape[0]
    out[height:] = rows[...].astype(bf16)
    out[:height] = qkv[...].astype(bf16)


def first_cast_pass(order, qkv, members):
    return order.call(
        functools.partial(first_cast_kernel, [member.size for member in members]),
        [qkv, jnp.concatenate(members)[None]],
        [in_vmem] * 2,
        [shape_of((qkv.shape[0] + 16, 3 * D), bf16)],
        [in_vmem],
        scratch=[pltpu.VMEM((16, 3 * D), f32)],
        limit=16,
        name="first_cast",
    )[0]


def cast_kernel(
    places,
    lengths,
    left,
    right,
    down,
    wide_out,
    down_out,
    lead_out,
    half_out,
    row_out,
    column_out,
):
    wide_out[:, :D] = left[...].astype(bf16)
    wide_out[:, D:] = right[...].astype(bf16)
    down_out[...] = down[...].astype(bf16)
    lead_out[...] = wide_out[:, : lead_out.shape[1]]
    rows = left.shape[0]
    turn = places[4] % 2
    first = turn * 2 * rows
    for run in range(2):
        start = pl.multiple_of(first + run * rows, 16)
        half_out[:rows, run * D : (run + 1) * D] = down_out[pl.ds(start, rows)]
    start = pl.multiple_of(turn * (rows // 2), 16)
    line = rows
    for column, width in RUNS:
        count = 2 * D // width
        height = rows // 2 // count
        for run in range(count):
            part = pl.ds(pl.multiple_of(start + run * height, 16), height)
            block = wide_out[part, D + column : D + column + width]
            half_out[line : line + height, run * width : (run + 1) * width] = block
        line += height
    pack = places[0] * 4 + places[4]
    row_places = lax.broadcasted_iota(jnp.int32, (1, SEQ), 1)
    column_places = lax.broadcasted_iota(jnp.int32, (SEQ, 1), 0)
    page_row, page_column = jnp.zeros_like(row_places), jnp.zeros_like(column_places)
    end = jnp.int32(0)
    for page in range(lengths.shape[1]):
        end += lengths[pack, page]
        page_row += (row_places >= end).astype(jnp.int32)
        page_column += (column_places >= end).astype(jnp.int32)
    row_out[...] = page_row
    column_out[...] = page_column


def cast_pass(order, places, lengths, left, right, down):
    rows = left.shape[0]
    return order.call(
        cast_kernel,
        [places, lengths, left, right, down],
        [in_smem] * 2 + [in_vmem] * 3,
        [
            shape_of((rows, D + FF), bf16),
            shape_of(down.shape, bf16),
            shape_of((rows, D + LEAD), bf16),
            shape_of((rows + sum(rows * width // (4 * D) for _, width in RUNS), 2 * D), bf16),
            shape_of((1, SEQ), jnp.int32),
            shape_of((SEQ, 1), jnp.int32),
        ],
        [in_vmem] * 6,
        limit=16,
        name="cast",
    )


def pairs_kernel(count, packed, places, rows, *rest):
    given, rest = ((), rest) if packed else (rest[:2], rest[2:])
    parts, rest = rest[:count], rest[count:]
    pair_outs, rest = rest[:GROUPS], rest[GROUPS:]
    normed_out, vectors_out, hidden_out, weight, wide_pair, last_pair, sems = rest
    pairs = [wide_pair.at[k] for k in range(GROUPS - 1)] + [last_pair]
    shard = D // count
    if packed:
        vectors = jnp.zeros((8, D), f32)
        line = lax.broadcasted_iota(jnp.int32, (8, D), 0)
        for k in range(count):
            block = parts[k][shard : shard + 16, :D].astype(f32)[:8]
            vectors += pltpu.roll(jnp.where(line < 7, block, 0.0), places[k] * shard, 1)
            start = pl.multiple_of(places[k] * D, 128)
            hidden_out[:, pl.ds(start, D)] = block[7:8]
    else:
        vectors = given[0][...]
        hidden_out[...] = given[1][...]
    vectors_out[...] = vectors
    for k, part in enumerate(parts):
        weight[pl.ds(pl.multiple_of(places[k] * shard, 16), shard)] = part[:shard, D:]
    scaled, _ = normalise(rows[...].astype(f32))
    normed_out[...] = (scaled * vectors[0:1] + vectors[1:2]).astype(bf16)
    for kind in range(2):
        line = vectors[6:7, kind * PART : (kind + 1) * PART]
        last_pair[kind, SEQ:] = jnp.concatenate([line] * 16, axis=0).astype(bf16)
    copies = []
    for group in range(GROUPS):
        for kind in range(2):
            first = kind * D + group * PART
            block = dot(normed_out[...], weight[:, first : first + PART])
            pairs[group][kind, :SEQ] = block.astype(bf16)
        copies.append(pltpu.make_async_copy(pairs[group], pair_outs[group], sems.at[group]))
        copies[-1].start()
    for copy in copies:
        copy.wait()


def pairs_pass(order, places, rows, parts, given=(), waits=()):
    count = len(parts)
    outs = order.call(
        functools.partial(pairs_kernel, count, not given),
        [places, rows, *given, *parts],
        [in_smem] + [in_vmem] * (1 + len(given) + count),
        [shape_of((2, SEQ, PART), bf16)] * (GROUPS - 1)
        + [
            shape_of((2, SEQ + 16, PART), bf16),
            shape_of((SEQ, D), bf16),
            shape_of((8, D), f32),
            shape_of((1, FF), f32),
        ],
        [in_hbm] * GROUPS + [in_vmem] * 3,
        scratch=[
            pltpu.VMEM((D, 2 * D), bf16),
            pltpu.VMEM((GROUPS - 1, 2, SEQ, PART), bf16),
            pltpu.VMEM((2, SEQ + 16, PART), bf16),
            pltpu.SemaphoreType.DMA((GROUPS,)),
        ],
        limit=16,
        name="pairs",
        waits=waits,
    )
    return outs[:GROUPS], *outs[GROUPS:]


def queries_kernel(places, normed, *rest):
    parts, (out, weight) = rest[:-2], rest[-2:]
    shard = D // len(parts)
    for k, part in enumerate(parts):
        weight[pl.ds(pl.multiple_of(places[k] * shard, 16), shard)] = part[:shard, :D]
    for first in range(0, D, PART):
        block = dot(normed[...], weight[:, first : first + PART])
        out[:, first : first + PART] = block.astype(bf16)


def queries_pass(order, places, normed, parts):
    return order.call(
        queries_kernel,
        [places, normed, *parts],
        [in_smem] + [in_vmem] * (1 + len(parts)),
        [shape_of((SEQ, D), bf16)],
        [in_vmem],
        scratch=[pltpu.VMEM((D, D), bf16)],
        limit=16,
        name="queries",
    )[0]


def fill_page_bias(page_row, page_column, bias):
    for index, (low, high) in enumerate(WINDOWS):
        start = index * BLOCK
        same = page_column[low:high] == page_row[:, start : start + BLOCK]
        bias[index, : high - low] = jnp.where(same, 0.0, masked_score)


def two_heads(block):
    lane = lax.broadcasted_iota(jnp.int32, block.shape, 1)
    zero = jnp.zeros_like(block)
    return jnp.concatenate(
        [jnp.where(lane < HEAD_DIM, block, zero), jnp.where(lane < HEAD_DIM, zero, block)], axis=0
    )


def head_rows(both):
    return jnp.concatenate([both[:HEAD_DIM, :BLOCK], both[HEAD_DIM:, BLOCK:]], axis=0).T


def page_bias(bias, index, size):
    block = bias[index, :size]
    return jnp.concatenate([block, block], axis=1)


def attend_kernel(
    query_first, query, own, other, page_row, page_column, context, log_total, bias
):
    fill_page_bias(page_row, page_column, bias)

    def exponents_of(step, index):
        low, high = WINDOWS[index]
        rows, lanes = slice(index * BLOCK, (index + 1) * BLOCK), slice(step * PAIR, (step + 1) * PAIR)
        query_lanes = slice((query_first + step) * PAIR, (query_first + step + 1) * PAIR)
        queries = two_heads(query[rows, query_lanes] * score_scale)
        allowed = page_bias(bias, index, high - low)
        scores = [dot_nt(side[0, low:high, lanes], queries) + allowed for side in (own, other)]
        largest = jnp.max(jnp.maximum(*scores), axis=0, keepdims=True)
        exponents = [jnp.exp(score - largest) for score in scores]
        total = column_sums(exponents[0] + exponents[1])
        log_total[step, index : index + 1] = largest + jnp.log(total)
        return exponents, 1.0 / total

    def context_of(step, index, found):
        exponents, inverse = found
        low, high = WINDOWS[index]
        rows, lanes = slice(index * BLOCK, (index + 1) * BLOCK), slice(step * PAIR, (step + 1) * PAIR)
        both = 0.0
        for side, exponent in zip((own, other), exponents):
            both += dot_tn(side[1, low:high, lanes], (exponent * inverse).astype(bf16))
        context[rows, lanes] = head_rows(both).astype(bf16)

    steps = [(k, w) for k in range(context.shape[1] // PAIR) for w in range(len(WINDOWS))]
    found = exponents_of(*steps[0])
    for place, now in enumerate(steps):
        ahead = exponents_of(*steps[place + 1]) if place + 1 < len(steps) else None
        context_of(*now, found)
        found = ahead


def attend(order, query_first, queries, own, other, page_row, page_column, waits=()):
    width = own.shape[2]
    return order.call(
        functools.partial(attend_kernel, query_first),
        [queries, own, other, page_row, page_column],
        [in_vmem] * 5,
        [
            shape_of((SEQ, width), bf16),
            shape_of((width // PAIR, len(WINDOWS), 2 * BLOCK), f32),
        ],
        [in_vmem] * 2,
        scratch=[pltpu.VMEM((len(WINDOWS), WINDOW, BLOCK), f32)],
        limit=12,
        name="attend",
        cost=60,
        waits=waits,
    )


def attend_back_kernel(
    query_first,
    query,
    own,
    other,
    context_grad,
    log_total,
    page_row,
    page_column,
    *rest,
):
    *given, query_grad, own_grad, other_grad, bias, other_sum = rest
    fill_page_bias(page_row, page_column, bias)
    own_grad[...] = jnp.zeros_like(own_grad)
    other_sum[...] = jnp.zeros_like(other_sum)

    def shares_of(step, index):
        low, high = WINDOWS[index]
        rows, lanes = slice(index * BLOCK, (index + 1) * BLOCK), slice(step * PAIR, (step + 1) * PAIR)
        query_lanes = slice((query_first + step) * PAIR, (query_first + step + 1) * PAIR)
        queries = two_heads(query[rows, query_lanes] * score_scale)
        grads = two_heads(context_grad[rows, query_lanes])
        offset = page_bias(bias, index, high - low) - log_total[step, index : index + 1]
        halves = []
        for side in (own, other):
            shares = jnp.exp(dot_nt(side[0, low:high, lanes], queries) + offset)
            halves.append((shares, dot_nt(side[1, low:high, lanes], grads)))
        centre = sum(column_sums(shares * share_grad) for shares, share_grad in halves)
        return queries, grads, halves, centre

    def grads_of(step, index, found):
        queries, grads, halves, centre = found
        low, high = WINDOWS[index]
        rows, lanes = slice(index * BLOCK, (index + 1) * BLOCK), slice(step * PAIR, (step + 1) * PAIR)
        both = 0.0
        for side, total, (shares, share_grad) in zip((own, other), (own_grad, other_sum), halves):
            score_grad = (shares * (share_grad - centre)).astype(bf16)
            total[1, low:high, lanes] += dot(shares.astype(bf16), grads)
            total[0, low:high, lanes] += dot(score_grad, queries)
            both += dot_tn(side[0, low:high, lanes], score_grad)
        query_grad[rows, lanes] = (head_rows(both) * score_scale).astype(bf16)

    steps = [(k, w) for k in range(own_grad.shape[2] // PAIR) for w in range(len(WINDOWS))]
    found = shares_of(*steps[0])
    for place, now in enumerate(steps):
        ahead = shares_of(*steps[place + 1]) if place + 1 < len(steps) else None
        grads_of(*now, found)
        found = ahead
    other_grad[:, :SEQ] = other_sum[...].astype(bf16)
    if given:
        for kind in range(2):
            line = given[0][:, kind * PART : (kind + 1) * PART]
            other_grad[kind, SEQ:] = jnp.concatenate([line] * 2, axis=0).astype(bf16)


def attend_back(
    order, query_first, queries, own, other, context_grad, logs, page_row, page_column, given
):
    return order.call(
        functools.partial(attend_back_kernel, query_first),
        [queries, own, other, context_grad, logs, page_row, page_column, *given],
        [in_vmem] * (7 + len(given)),
        [
            shape_of((SEQ, PART), bf16),
            shape_of((2, SEQ, PART), f32),
            shape_of((2, SEQ + 16 * len(given), PART), bf16),
        ],
        [in_vmem] * 3,
        scratch=[
            pltpu.VMEM((len(WINDOWS), WINDOW, BLOCK), f32),
            pltpu.VMEM((2, SEQ, PART), f32),
        ],
        limit=16,
        name="attend_back",
        cost=60,
    )


def partner_cross(pair):
    rows = pair[:, SEQ:].astype(f32)
    return jnp.concatenate([rows[0, :1], rows[1, :1]], axis=1)


def join_blocks(places, wides, downs, leads, halves, wide, down):
    rows = wide.shape[0] // (len(wides) + len(leads))
    for k, part in enumerate(wides):
        wide[pl.ds(pl.multiple_of(places[k] * rows, 16), rows)] = part[...]
        down[k] = downs[k][...]
    turn = places[4] % 2
    for k, part in enumerate(leads):
        first = places[len(wides) + k] * rows
        wide[pl.ds(pl.multiple_of(first, 16), rows), : part.shape[1]] = part[...]
        for side, half in enumerate(halves[k]):
            place = turn if side == 0 else 1 - turn
            line = rows
            for column, width in RUNS:
                runs = 2 * D // width
                height = rows // 2 // runs
                for run in range(runs):
                    start = pl.multiple_of(first + place * (rows // 2) + run * height, 16)
                    block = half[line : line + height, run * width : (run + 1) * width]
                    wide[pl.ds(start, height), D + column : D + column + width] = block
                line += height
            for run in range(2):
                start = pl.multiple_of((2 * place + run) * rows, 16)
                down[len(wides) + k, pl.ds(start, rows)] = half[:rows, run * D : (run + 1) * D]


def middle_kernel(kinds, places, rows, *rest):
    contexts, rest = rest[:GROUPS], rest[GROUPS:]
    (tangent, vectors, partner, hidden_bias), rest = rest[:4], rest[4:]
    wides, downs, leads = [], [], []
    for group, size in zip((wides, downs, leads), kinds):
        group += rest[:size]
        rest = rest[size:]
    halves = [rest[2 * k : 2 * k + 2] for k in range(kinds[2])]
    rest = rest[2 * kinds[2] :]
    middle_out, second_out, hidden_out, slope_out, modal_out, inner_out, wide, down, total = rest
    join_blocks(places, wides, downs, leads, halves, wide, down)
    count = down.shape[0]
    middle = rows[...].astype(f32)
    for group, context in enumerate(contexts):
        middle += dot(context[...], wide[group * PART : (group + 1) * PART, :D])
    middle_out[...] = middle
    scaled, _ = normalise(middle)
    second_out[...] = (scaled * vectors[2:3] + vectors[3:4]).astype(bf16)
    total[...] = middle + vectors[4:5]
    slot = FF // count
    size = 768
    def upper_of(k, first):
        start = places[k] * slot + first
        part = pl.ds(pl.multiple_of(start, 128), size)
        column = pl.ds(pl.multiple_of(D + start, 128), size)
        return part, dot(second_out[...], wide[:, column]) + hidden_bias[:, part]

    steps = [(k, first) for k in range(count) for first in range(0, slot, size)]
    found = upper_of(*steps[0])
    for place, (k, first) in enumerate(steps):
        ahead = upper_of(*steps[place + 1]) if place + 1 < len(steps) else None
        part, upper = found
        square = upper * upper
        angle = jnp.tanh(upper * (gelu_scale + (gelu_cubic * gelu_scale) * square))
        half = 0.5 + 0.5 * angle
        hidden = (upper * half).astype(bf16)
        hidden_out[:, part] = hidden
        bend = 2.0 * gelu_scale + (6.0 * gelu_cubic * gelu_scale) * square
        slope_out[:, part] = (half + half * (1.0 - half) * (upper * bend)).astype(bf16)
        total[...] += dot(hidden, down[k, first : first + size])
        found = ahead
    modal_out[...] = total[...].astype(bf16)
    modal = modal_out[...].astype(f32)
    own = jnp.sum(modal * vectors[5:6], axis=1, keepdims=True)
    cross = jnp.sum(modal * partner_cross(partner), axis=1, keepdims=True)
    met = jnp.sum(modal * tangent[...].astype(f32), axis=1, keepdims=True)
    lane = lax.broadcasted_iota(jnp.int32, (SEQ, 128), 1)
    columns = jnp.where(lane == 0, own, jnp.where(lane == 1, cross, met))
    inner_out[...] = columns.T[:8]


def middle_pass(
    order, places, rows, contexts, tangent, vectors, partner, hidden_bias, wides, downs, leads, halves
):
    count = len(wides) + len(leads)
    parts = [*wides, *downs, *leads] + [piece for pair in halves for piece in pair]
    return order.call(
        functools.partial(middle_kernel, (len(wides), len(downs), len(leads))),
        [places, rows, *contexts, tangent, vectors, partner, hidden_bias, *parts],
        [in_smem] + [in_vmem] * (5 + GROUPS + len(parts)),
        [
            shape_of((SEQ, D), f32),
            shape_of((SEQ, D), bf16),
            shape_of((SEQ, FF), bf16),
            shape_of((SEQ, FF), bf16),
            shape_of((SEQ, D), bf16),
            shape_of((8, SEQ), f32),
            shape_of((D, D + FF), bf16),
            shape_of((count, FF // count, D), bf16),
        ],
        [in_vmem] * 8,
        scratch=[pltpu.VMEM((SEQ, D), f32)],
        limit=16,
        name="middle",
    )


def gate_kernel(
    own,
    other,
    tangent,
    partner_tangent,
    vectors,
    partner,
    grad_out,
    low_out,
    columns_out,
    sums,
):
    gate = jax.nn.sigmoid(own[0:1] + other[1:2])
    gate_two = jax.nn.sigmoid(other[0:1] + own[1:2])
    logit = other[2:3] * gate * (1.0 - gate)
    logit_two = own[2:3] * gate_two * (1.0 - gate_two)
    padding = jnp.zeros((124, SEQ), f32)
    columns = jnp.concatenate([gate, logit, gate_two, logit_two, padding], axis=0).T
    columns_out[...] = columns
    grad = (
        tangent[...].astype(f32)
        + columns[:, 1:2] * vectors[5:6]
        + partner_tangent[...].astype(f32) * columns[:, 2:3]
        + columns[:, 3:4] * partner_cross(partner)
    )
    grad_out[...] = grad
    low_out[...] = grad.astype(bf16)
    sums[...] = column_sums(grad)


def gate_pass(order, own, other, tangent, partner_tangent, vectors, partner):
    return order.call(
        gate_kernel,
        [own, other, tangent, partner_tangent, vectors, partner],
        [in_vmem] * 6,
        [
            shape_of((SEQ, D), f32),
            shape_of((SEQ, D), bf16),
            shape_of((SEQ, 128), f32),
            shape_of((1, D), f32),
        ],
        [in_vmem] * 4,
        name="gate",
    )


def mix_kernel(own, other, columns, mixed):
    mixed[...] = (
        own[...].astype(f32) + columns[:, 0:1] * other[...].astype(f32)
    ).astype(bf16)


def mix_pass(order, own, other, columns, waits=()):
    return order.call(
        mix_kernel,
        [own, other, columns],
        [in_vmem] * 3,
        [shape_of((SEQ, D), bf16)],
        [in_vmem],
        name="mix",
        cost=60,
        waits=waits,
    )[0]


def gate_sums_kernel(own, columns, out):
    rows = own[...].astype(f32)
    out[...] = jnp.zeros_like(out)
    out[0:1] = column_sums(columns[:, 1:2] * rows)
    out[1:2] = column_sums(columns[:, 3:4] * rows)


def gate_sums_pass(order, own, columns):
    return order.call(
        gate_sums_kernel, [own, columns], [in_vmem] * 2, [shape_of((8, D), f32)], [in_vmem], name="gate_sums"
    )[0]


def chain_kernel(places, low, grad, slope, middle, vectors, wide, down, *rest):
    total_out, total_low_out, context_out, upper_out, upper_sums, gain_sums, bias_sums = rest[:7]
    normed_grad = rest[7]
    normed_grad[...] = jnp.zeros_like(normed_grad)
    count = down.shape[0]
    slot = FF // count
    size = 768
    def upper_of(k, first):
        start = places[k] * slot + first
        part = pl.ds(pl.multiple_of(start, 128), size)
        column = pl.ds(pl.multiple_of(D + start, 128), size)
        return part, column, dot_nt(low[...], down[k, first : first + size])

    steps = [(k, first) for k in range(count) for first in range(0, slot, size)]
    found = upper_of(*steps[0])
    for place in range(len(steps)):
        ahead = upper_of(*steps[place + 1]) if place + 1 < len(steps) else None
        part, column, upper = found
        upper = upper * slope[:, part].astype(f32)
        upper_sums[:, part] = column_sums(upper)
        upper_low = upper.astype(bf16)
        upper_out[:, part] = upper_low
        normed_grad[...] += dot_nt(upper_low, wide[:, column])
        found = ahead
    scaled, root = normalise(middle[...])
    incoming = normed_grad[...]
    gain_sums[...] = column_sums(incoming * scaled)
    bias_sums[...] = column_sums(incoming)
    total = grad[...] + norm_back(scaled, root, vectors[2:3], incoming)
    total_out[...] = total
    total_low_out[...] = total.astype(bf16)
    context_out[...] = dot_nt(total_low_out[...], wide[:, :D]).astype(bf16)


def chain_pass(order, places, low, grad, slope, middle, vectors, wide, down):
    return order.call(
        chain_kernel,
        [places, low, grad, slope, middle, vectors, wide, down],
        [in_smem] + [in_vmem] * 7,
        [
            shape_of((SEQ, D), f32),
            shape_of((SEQ, D), bf16),
            shape_of((SEQ, D), bf16),
            shape_of((SEQ, FF), bf16),
            shape_of((1, FF), f32),
            shape_of((1, D), f32),
            shape_of((1, D), f32),
        ],
        [in_vmem] * 7,
        scratch=[pltpu.VMEM((SEQ, D), f32)],
        limit=20,
        name="chain",
    )


def slots_of(count):
    return (list(range(0, count, 2)), list(range(1, count, 2)))


def block_shapes(widths, count):
    near, far = slots_of(count)
    rows = D // count
    outs = []
    for width in widths:
        outs.append(shape_of((len(near), rows, width), bf16))
        if far:
            outs.append(shape_of((len(far), rows, width), bf16))
    return outs


def store_blocks(places, count, products, widths, outs, whole):
    near, far = slots_of(count)
    rows = D // count
    products = list(products)
    each = 2 if far else 1
    for index, width in enumerate(widths):
        low = 0
        while low < width:
            left, right = products.pop(0)
            whole[:, low : low + right.shape[1]] = dot(left, right).astype(bf16)
            low += right.shape[1]
        for out, slots in zip(outs[each * index : each * index + each], (near, far)):
            for place, slot in enumerate(slots):
                begin = pl.multiple_of(places[slot] * rows, 16)
                out[place] = whole[pl.ds(begin, rows), :width]


def up_grads_kernel(count, widths, places, second, upper, *rest):
    turned = second[...].T
    products = [(turned, upper[:, k : k + 512]) for k in range(0, FF, 512)]
    store_blocks(places, count, products, widths, rest[:-1], rest[-1])


def up_grads(order, places, second, upper, widths, count):
    outs = block_shapes(widths, count)
    return order.call(
        functools.partial(up_grads_kernel, count, widths),
        [places, second, upper],
        [in_smem] + [in_vmem] * 2,
        outs,
        [in_vmem] * len(outs),
        scratch=[pltpu.VMEM((D, max(widths)), bf16)],
        limit=16,
        name="up_grads",
    )


def lead_grads_kernel(count, places, context, context_two, low, normed, *rest):
    queries, (own, returned), rest = rest[:GROUPS], rest[GROUPS : GROUPS + 2], rest[GROUPS + 2 :]
    pair_low, outs, whole = rest[0], rest[1:-1], rest[-1]
    pair_low[...] = (own[...] + returned[:, :SEQ].astype(f32)).astype(bf16)
    turned = jnp.concatenate([context[...].T, context_two[...].T], axis=0)
    products = [(turned, low[:, k : k + PART]) for k in range(0, D, PART)]
    turned = normed[...].T
    products += [(turned, query[...]) for query in queries]
    products += [(turned, pair_low[kind]) for kind in range(2)]
    store_blocks(places, count, products, [3 * D], outs, whole)


def lead_grads(order, places, contexts, low, normed, queries, own, returned, count):
    outs = block_shapes([3 * D], count)
    args = [*contexts, low, normed, *queries, own, returned]
    return order.call(
        functools.partial(lead_grads_kernel, count),
        [places, *args],
        [in_smem] + [in_vmem] * len(args),
        [shape_of(own.shape, bf16)] + outs,
        [in_vmem] * (1 + len(outs)),
        scratch=[pltpu.VMEM((D, 3 * D), bf16)],
        limit=16,
        name="lead_grads",
    )


def down_grads_kernel(count, first, height, fold, places, low, hidden, *outs):
    near, far = slots_of(count)
    width = FF // count
    turned = low[:, first : first + height].T
    rows = height // fold
    for out, slots in zip(outs, (near, far)):
        for place, slot in enumerate(slots):
            begin = pl.multiple_of(places[slot] * width, 128)
            block = dot(turned, hidden[:, pl.ds(begin, width)]).astype(bf16)
            for k in range(fold):
                out[place, :, k * width : (k + 1) * width] = block[k * rows : (k + 1) * rows]


def down_grads(order, places, low, hidden, first, height, fold, count):
    near, far = slots_of(count)
    width = FF // count
    outs = [shape_of((len(near), height // fold, fold * width), bf16)]
    if far:
        outs.append(shape_of((len(far), height // fold, fold * width), bf16))
    return order.call(
        functools.partial(down_grads_kernel, count, first, height, fold),
        [places, low, hidden],
        [in_smem, in_vmem, in_vmem],
        outs,
        [in_vmem] * len(outs),
        limit=16,
        name="down_grads",
    )


def first_kernel(count, places, total, rows, vectors, normed, own, returned, *rest):
    parts, rest = rest[:count], rest[count:]
    queries, pair, rest = rest[:GROUPS], rest[GROUPS], rest[GROUPS + 1 :]
    gain_two, bias_two, output_bias, gate_own, hidden_bias = rest[:5]
    grad_out, outs = rest[5], rest[6:-5]
    pair_low, normed_grad, weight, whole, short = rest[-5:]
    pair_low[...] = (own[...] + returned[:, :SEQ].astype(f32)).astype(bf16)
    assemble(places, parts, weight)
    for group, pairs in enumerate((pair, pair_low)):
        start = group * PART
        block = dot_nt(queries[group][...], weight[:, start : start + PART])
        for kind in range(2):
            start = (kind + 1) * D + group * PART
            block += dot_nt(pairs[kind], weight[:, start : start + PART])
        if group == 0:
            normed_grad[...] = block
        else:
            normed_grad[...] += block
    scaled, root = normalise(rows[...].astype(f32))
    incoming = normed_grad[...]
    short[...] = jnp.zeros_like(short)
    short[0:1] = column_sums(incoming * scaled)
    short[1:2] = column_sums(incoming)
    for line, member in enumerate((gain_two, bias_two, output_bias)):
        short[line + 2 : line + 3] = member[...]
    short[5:6] = gate_own[0:1]
    for kind in range(2):
        line = returned[kind, SEQ : SEQ + 8].astype(f32)
        short[6:7, kind * PART : (kind + 1) * PART] = line[1:2]
    for line in range(FF // D):
        short[line + 8 : line + 9] = hidden_bias[:, line * D : (line + 1) * D]
    grad_out[...] = total[...] + norm_back(scaled, root, vectors[0:1], incoming)
    turned = normed[...].T
    for kind in range(2):
        whole[:, kind * PART : (kind + 1) * PART] = dot(turned, pair_low[kind]).astype(bf16)
    height = D // count
    for out, slots in zip(outs, slots_of(count)):
        for place, slot in enumerate(slots):
            begin = pl.multiple_of(places[slot] * height, 16)
            out[place * height : (place + 1) * height] = whole[pl.ds(begin, height)]
        out[len(slots) * height :] = short[...].astype(bf16)


def first_pass(
    order, places, total, rows, vectors, normed, own, returned, parts, queries, pair, short
):
    count = len(parts)
    args = [total, rows, vectors, normed, own, returned, *parts, *queries, pair, *short]
    outs = [
        shape_of((len(slots) * (D // count) + 16, 2 * PART), bf16) for slots in slots_of(count) if slots
    ]
    return order.call(
        functools.partial(first_kernel, count),
        [places, *args],
        [in_smem] + [in_vmem] * len(args),
        [shape_of((SEQ, D), f32)] + outs,
        [in_vmem] * (1 + len(outs)),
        scratch=[
            pltpu.VMEM((2, SEQ, PART), bf16),
            pltpu.VMEM((SEQ, D), f32),
            pltpu.VMEM((D, 3 * D), bf16),
            pltpu.VMEM((D, 2 * PART), bf16),
            pltpu.VMEM((16, D), f32),
        ],
        limit=20,
        name="first",
    )


def settle_kernel(kind, count, outs, places, *refs):
    totals, returned, refs = refs[:count], refs[count : 2 * count], refs[2 * count :]
    targets, (scratch, sems) = refs[:outs], (refs[outs : 2 * outs], refs[2 * outs])
    copies = []

    def leave(index, *where):
        source, target = scratch[index].at[where], targets[index].at[where]
        copies.append(pltpu.make_async_copy(source, target, sems.at[len(copies)]))
        copies[-1].start()

    inner = jnp.logical_and(places[4] > 0, places[4] < 3)
    values = [jnp.where(inner, a[...], b[...]).astype(f32) for a, b in zip(totals, returned)]
    out, every = scratch[0], slice(None)
    if kind == "turn":
        first = 0
        for value in values:
            rows = value.shape[0]
            start = first
            for k in range(0, value.shape[1], D):
                out[:, first : first + rows] = value[:, k : k + D].T
                first += rows
            leave(0, every, pl.ds(start, first - start))
    elif kind == "columns":
        first = 0
        for value in values:
            out[:, first : first + value.shape[1]] = value
            leave(0, every, pl.ds(first, value.shape[1]))
            first += value.shape[1]
    else:
        scratch[1][...] = values[0][:, :D]
        leave(1, every)
        out[:, :D] = values[0][:, D:]
        for group, value in enumerate(values[1:]):
            for part in range(2):
                start = (part + 1) * D + group * PART
                out[:, start : start + PART] = value[:, part * PART : (part + 1) * PART]
        leave(0, every)
    for copy in copies:
        copy.wait()


def settle(order, kind, places, blocks, dims):
    count = len(blocks)
    found = order.call(
        functools.partial(settle_kernel, kind, count, len(dims)),
        [places] + [block[0] for block in blocks] + [block[1] for block in blocks],
        [in_smem] + [in_vmem] * (2 * count),
        [shape_of(each, f32) for each in dims],
        [in_hbm] * len(dims),
        scratch=[pltpu.VMEM(each, f32) for each in dims] + [pltpu.SemaphoreType.DMA((8,))],
        name="settle",
    )
    return found[0] if len(dims) == 1 else found


def last_settle_kernel(places, total, returned, given, out, *rest):
    short_outs, (scratch, sems) = rest[:8], rest[8:]
    inner = jnp.logical_and(places[4] > 0, places[4] < 3)
    value = jnp.where(inner, total[...], returned[...]).astype(f32)
    rows = scratch.shape[1]
    copies = []
    for part in range(2):
        scratch[part] = value[:rows, part * PART : (part + 1) * PART]
        place = out.at[:, pl.ds((part + 1) * D + PART, PART)]
        copies.append(pltpu.make_async_copy(scratch.at[part], place, sems.at[part]))
        copies[-1].start()
    short = value[rows:]
    turned = pltpu.roll(short, D - places[0] * rows, 1)
    for line in range(7):
        short_outs[line][...] = turned[line : line + 1, :rows].reshape(rows)
    line = lax.broadcasted_iota(jnp.int32, short.shape, 0)
    hidden = jnp.sum(jnp.where(line == 8 + places[0], short, 0.0), axis=0)
    short_outs[7][...] = hidden
    for copy in copies:
        copy.wait()


def last_settle(order, places, block, given):
    rows = given.shape[0]
    shorts = [shape_of((rows,), f32)] * 7 + [shape_of((D,), f32)]
    found = order.call(
        last_settle_kernel,
        [places, block[0], block[1], given],
        [in_smem, in_vmem, in_vmem, in_hbm],
        [shape_of(given.shape, f32)] + shorts,
        [in_hbm] + [in_vmem] * 8,
        scratch=[pltpu.VMEM((2, rows, PART), f32), pltpu.SemaphoreType.DMA((2,))],
        name="last_settle",
        aliases={3: 0},
    )
    return found[0], found[1:]


def swap_bit(value, axis, bit):
    size = lax.axis_size(axis)
    return lax.ppermute(value, axis, [(source, source ^ (1 << bit)) for source in range(size)])


def from_partner(value):
    size = lax.axis_size("stream")
    half = size // 2
    return lax.ppermute(value, "stream", [(source, (source + half) % size) for source in range(size)])


def along(value, pairs):
    return lax.ppermute(value, "dp", pairs)


def up_line(value, steps):
    return along(value, [(floor, floor + 1) for floor in range(steps - 1, 3)])


def down_line(value, steps):
    return along(value, [(floor, floor - 1) for floor in range(1, 5 - steps)])


def swap_outer(value):
    return along(value, [(0, 1), (1, 0), (2, 3), (3, 2)])


def to_inner(value):
    return along(value, [(0, 1), (3, 2)])


def over_middle(value):
    return along(value, [(1, 2), (2, 1)])


def to_outer(value):
    return along(value, [(1, 0), (2, 3)])


def core(value):
    return swap_bit(value, "stream", 0)


def across(value):
    return swap_bit(value, "stream", 1)


def modality_groups():
    size = lax.axis_size("stream")
    half = size // 2
    return [list(range(half)), list(range(half, size))]


def body(
    regions,
    cotangent,
    page_lens,
    qkv_weight,
    out_weight,
    up_weight,
    down_weight,
    ln1_gain,
    ln1_bias,
    ln2_gain,
    ln2_bias,
    up_bias,
    down_bias,
    gate_own,
    gate_other,
):
    half = lax.axis_size("stream") // 2
    depth = lax.axis_size("dp")
    paired = half == 4 and depth == 4
    side = lax.axis_index("stream") % half
    floor = lax.axis_index("dp")
    count = 4 if paired else 1
    slots = jnp.arange(4, dtype=jnp.int32)
    picks = jnp.bitwise_xor(side.astype(jnp.int32), slots) if paired else jnp.zeros_like(slots)
    places = jnp.concatenate([picks, floor.astype(jnp.int32)[None]])
    order = Order()
    short = (ln1_gain, ln1_bias, ln2_gain, ln2_bias, down_bias, gate_own, gate_other, up_bias)
    partner_tangent = from_partner(cotangent)

    def attend_group(group, waits=()):
        context, log_total = attend(
            order,
            group * PART // PAIR,
            queries,
            own_pairs[group],
            other_pairs[group],
            page_row,
            page_column,
            waits,
        )
        contexts.append(context)
        logs.append(log_total)

    contexts, logs = [], []
    if paired:
        qkv_shard = first_cast_pass(order, qkv_weight, short)
        qkv_across, qkv_near = across(qkv_shard), core(qkv_shard)
        wide_shard, down_shard, lead, half_own, page_row, page_column = cast_pass(
            order, places, page_lens, out_weight, up_weight, down_weight
        )
        wide_near, down_near = core(wide_shard), core(down_shard)
        (qkv_across,) = order.hold([qkv_across], waits=[partner_tangent, qkv_near])
        qkv_far, half_own = core(qkv_across), across(half_own)
        qkv_parts = [qkv_shard, qkv_near, qkv_across, qkv_far]
        own_pairs, normed, vectors, hidden_bias = pairs_pass(
            order, places, regions, qkv_parts, waits=[wide_near, down_near]
        )
        queries = queries_pass(order, places, normed, qkv_parts)
        other_pairs = [from_partner(pair) for pair in own_pairs]
        lead_across = across(lead)
        (half_own,) = order.hold([half_own])
        half_other, half_own_far = swap_outer(half_own), core(half_own)
        attend_group(0)
        (lead_across,) = order.hold([lead_across])
        vectors = order.pause(vectors)
        (half_other,) = order.hold([half_other])
        half_other_far, lead_far = core(half_other), core(lead_across)
        attend_group(1)
        wides, downs = [wide_shard, wide_near], [down_shard, down_near]
        leads = [lead_across, lead_far]
        halves = [(half_own, half_other), (half_own_far, half_other_far)]
    else:
        lengths = lax.dynamic_slice_in_dim(page_lens, side * depth + floor, 1, 0)
        positions = jnp.arange(SEQ, dtype=jnp.int32)
        page_ends = jnp.cumsum(lengths[0], dtype=jnp.int32)
        pages = jnp.sum((page_ends[:, None] <= positions[None, :]).astype(jnp.int32), axis=0)
        page_row, page_column = pages[None, :], pages[:, None]

        def gather(shard):
            return [
                lax.all_gather(shard, "stream", axis_index_groups=modality_groups(), tiled=True)
            ]

        packed = jnp.concatenate([member.astype(bf16) for member in short])[None]
        found = gather(packed)[0].astype(f32)
        shard = D // half
        rows = [found[:, k * shard : (k + 1) * shard].reshape(1, D) for k in range(7)]
        given = (
            jnp.concatenate(rows + [jnp.zeros((1, D), f32)], axis=0),
            found[:, 7 * shard :].reshape(1, FF),
        )
        qkv_parts = gather(qkv_weight.astype(bf16))
        wides = gather(jnp.concatenate([out_weight, up_weight], axis=1).astype(bf16))
        downs, leads, halves = gather(down_weight.astype(bf16)), [], []
        own_pairs, normed, vectors, hidden_bias = pairs_pass(
            order, places, regions, qkv_parts, given
        )
        queries = queries_pass(order, places, normed, qkv_parts)
        other_pairs = [from_partner(pair) for pair in own_pairs]
        for group in range(GROUPS):
            attend_group(group)

    middle, second, hidden, slope, modal, inner_own, wide, down = middle_pass(
        order,
        places,
        regions,
        contexts,
        partner_tangent,
        vectors,
        other_pairs[-1],
        hidden_bias,
        wides,
        downs,
        leads,
        halves,
    )
    inner_other = from_partner(inner_own)
    modal_grad, modal_low, columns, output_bias_grad = gate_pass(
        order, inner_own, inner_other, cotangent, partner_tangent, vectors, other_pairs[-1]
    )

    def attend_back_group(group):
        query_grad, own_grad, other_grad = attend_back(
            order,
            group * PART // PAIR,
            queries,
            own_pairs[group],
            other_pairs[group],
            context_grad,
            logs[group],
            page_row,
            page_column,
            [gate_sums] if group == GROUPS - 1 else [],
        )
        query_grads.append(query_grad)
        own_grads.append(own_grad)
        returned.append(from_partner(other_grad))

    def last_pass(pair_low):
        short_grads = (
            gain_two_grad,
            bias_two_grad,
            output_bias_grad,
            gate_sums,
            hidden_bias_grad,
        )
        return first_pass(
            order,
            places,
            middle_grad,
            regions,
            vectors,
            normed,
            own_grads[1],
            returned[1],
            qkv_parts,
            query_grads,
            pair_low,
            short_grads,
        )

    query_grads, own_grads, returned = [], [], []
    back = (order, places, modal_low, modal_grad, slope, middle, vectors, wide, down)
    if paired:
        d1, far = down_grads(order, places, modal_low, hidden, 0, 384, 2, count)
        d1_core = core(far)
        d2, far = down_grads(order, places, modal_low, hidden, 384, 384, 2, count)
        d2_core = core(far)
        d1, away = sums_pass(order, places, folds=[(d1, d1_core, [FF // 2])])
        d1_in = across(away)
        d2, d2_away = sums_pass(order, places, folds=[(d2, d2_core, [FF // 2])])
        middle_grad, middle_low, context_grad, upper_low, *rest = chain_pass(*back)
        hidden_bias_grad, gain_two_grad, bias_two_grad = rest
        d1 = sums_pass(order, places, adds=[(d1, d1_in)])
        d1_in = to_inner(d1)
        (d2_away,) = order.hold([d2_away])
        d2_in = across(d2_away)
        gate_sums = gate_sums_pass(order, modal, columns)
        u1, far_one, u2, far_two = up_grads(
            order, places, second, upper_low, [FF // 2, FF // 2], count
        )
        u1_core, u2_core = core(far_one), core(far_two)
        attend_back_group(0)
        d2, d1 = sums_pass(order, places, adds=[(d2, d2_in), (d1, d1_in)])
        d2_in, d1_mid = to_inner(d2), over_middle(d1)
        columns = order.pause(columns)
        u1, away = sums_pass(order, places, folds=[(u1, u1_core, [FF // 2])])
        u1_in = across(away)
        u2, away = sums_pass(order, places, folds=[(u2, u2_core, [FF // 2])])
        attend_back_group(1)
        d2, u1, u1_pay = sums_pass(
            order, places, adds=[(d2, d2_in)], pays=[(u1, u1_in, d1, d1_mid)]
        )
        u1_in, d2_mid = swap_outer(u1_pay), over_middle(d2)
        (away,) = order.hold([away])
        u2_in = across(away)
        pair_low, lead_near, lead_far = lead_grads(
            order, places, contexts, middle_low, normed, query_grads, own_grads[0], returned[0], count
        )
        lead_core = core(lead_far)
        u1, u2, u2_pay = sums_pass(
            order, places, adds=[(u1, u1_in)], pays=[(u2, u2_in, d2, d2_mid)]
        )
        d1_out = u1_in
        u2_in, u1_mid = swap_outer(u2_pay), over_middle(u1)
        gate_sums = order.pause(gate_sums)
        oq, away, p1, away_two = sums_pass(
            order, places, folds=[(lead_near, lead_core, [2 * D, D])]
        )
        oq_in = across(away)
        region_grad, last_near, last_far = last_pass(pair_low)
        last_core = core(last_far)
        u2, oq, oq_pay = sums_pass(
            order, places, adds=[(u2, u2_in)], pays=[(oq, oq_in, u1, u1_mid)]
        )
        d2_out = u2_in
        oq_in, u2_mid = swap_outer(oq_pay), over_middle(u2)
        (away_two,) = order.hold([away_two])
        p1_in = across(away_two)
        modal = order.pause(modal)
        p2, away = sums_pass(order, places, folds=[(last_near, last_core, [D])])
        p2_in = across(away)
        down_grad = settle(order, "turn", places, [(u1_pay, d1_out), (u2_pay, d2_out)], [(D, D)])
        oq, u2, p1 = sums_pass(
            order, places, adds=[(oq, oq_in), (u2, u2_mid), (p1, p1_in)]
        )
        u1_out = oq_in
        oq_mid, u2_out, p1_in = over_middle(oq), to_outer(u2), to_inner(p1)
        p2 = sums_pass(order, places, adds=[(p2, p2_in)])
        p2_in = to_inner(p2)
        p1 = sums_pass(order, places, adds=[(p1, p1_in)])
        p1_mid = over_middle(p1)
        (modal,) = order.hold([modal])
        partner_modal = from_partner(modal)
        oq, p2 = sums_pass(order, places, adds=[(oq, oq_mid), (p2, p2_in)], waits=[u2_out])
        oq_out, p2_mid = to_outer(oq), over_middle(p2)
        up_grad = settle(order, "columns", places, [(oq_pay, u1_out), (u2, u2_out)], [(D // 4, FF)])
        p1 = sums_pass(order, places, adds=[(p1, p1_mid)])
        p1_out = to_outer(p1)
        p2 = sums_pass(order, places, adds=[(p2, p2_mid)])
        p2_out = to_outer(p2)
        mixed_rows = mix_pass(order, modal, partner_modal, columns, [oq_out])
        qkv_grad, out_grad = settle(
            order,
            "pairs",
            places,
            [(oq, oq_out), (p1, p1_out)],
            [(D // 4, 3 * D), (D // 4, D)],
        )
        qkv_grad, shorts = last_settle(order, places, (p2, p2_out), qkv_grad)
    else:
        (down_block,) = down_grads(order, places, modal_low, hidden, 0, D, 1, count)
        middle_grad, middle_low, context_grad, upper_low, *rest = chain_pass(*back)
        hidden_bias_grad, gain_two_grad, bias_two_grad = rest
        (up_block,) = up_grads(order, places, second, upper_low, [FF], count)
        gate_sums = gate_sums_pass(order, modal, columns)
        for group in range(GROUPS):
            attend_back_group(group)
        mixed_rows = mix_pass(order, modal, from_partner(modal), columns)
        pair_low, lead_block = lead_grads(
            order, places, contexts, middle_low, normed, query_grads, own_grads[0], returned[0], count
        )
        region_grad, last_block = last_pass(pair_low)
        lead_block = lead_block[0]
        short_rows = last_block[D:].astype(f32)

        def total(block):
            groups = modality_groups()
            owned = lax.psum_scatter(
                block.astype(f32), "stream", axis_index_groups=groups, tiled=True
            )
            return lax.psum(owned, "dp")

        down_grad = total(down_block[0].T)
        up_grad, out_grad = total(up_block[0]), total(lead_block[:, :D])
        qkv_grad = total(
            jnp.concatenate(
                [
                    lead_block[:, D : 2 * D + PART],
                    last_block[:D, :PART],
                    lead_block[:, 2 * D + PART :],
                    last_block[:D, PART:],
                ],
                axis=1,
            )
        )
        short_rows = lax.psum(
            lax.psum(short_rows, "stream", axis_index_groups=modality_groups()), "dp"
        )

        shard = D // half
        own_rows = lax.dynamic_slice_in_dim(short_rows, side * shard, shard, 1)
        hidden_rows = short_rows[8 : 8 + FF // D].reshape(FF)
        own_hidden = lax.dynamic_slice_in_dim(hidden_rows, side * (FF // half), FF // half, 0)
        shorts = [own_rows[k] for k in range(7)] + [own_hidden]
    return (
        mixed_rows,
        region_grad,
        qkv_grad,
        out_grad,
        up_grad,
        down_grad,
        shorts[0],
        shorts[1],
        shorts[2],
        shorts[3],
        shorts[7],
        shorts[4],
        shorts[5],
        shorts[6],
    )


def solution(mesh):
    in_specs = (
        P(("stream", "dp"), None),
        P(("stream", "dp"), None),
        P(),
        P("stream", None),
        P("stream", None),
        P("stream", None),
        P("stream", None),
        P("stream"),
        P("stream"),
        P("stream"),
        P("stream"),
        P("stream"),
        P("stream"),
        P("stream"),
        P("stream"),
    )
    out_specs = (
        P(("stream", "dp"), None),
        P(("stream", "dp"), None),
        P("stream", None),
        P("stream", None),
        P("stream", None),
        P("stream", None),
        P("stream"),
        P("stream"),
        P("stream"),
        P("stream"),
        P("stream"),
        P("stream"),
        P("stream"),
        P("stream"),
    )
    return jax.shard_map(body, mesh=mesh, in_specs=in_specs, out_specs=out_specs, check_vma=False)
```

profile of v0, /device:TPU:0, one launch (start us, length us, event | category | flops | bytes accessed | tf_op | source)
XLA Modules:
  0.0 243.6 jit_solution(14980709073397500937)
XLA Ops:
  3.1 3.0 %collective-permute-start.1 = (bf16[208,2304]{1,0:T(8,128)(2,1)S(1)}, bf16[208,2304]{1,0:T(8,128)(2,1)S(1)}, u32[]{:S(2)}, u32[]{:S(2)}) collective-permute-start(bf16[208,2304]{1,0:T(8,128)(2,1)S(1)} %get-tuple-element.151.refs_2_.refs_7_), channel_id=1, source_target_pairs={{0,8},{4,12},{8,0},{12,4},{16,24},{20,28},{24,16},{28,20},{1,9},{5... | collective-permute-start | bytes 2875400 | tf_op jit(solution)/shard_map/ppermute | solution.py:1088
  7.8 1.7 copy-done.11
  9.4 1.7 copy-done.12
  11.1 1.8 cast.1
  13.5 12.9 %collective-permute-done.2.refs_2_.refs_4_.refs_3_ = bf16[512,768]{1,0:T(8,128)(2,1)} collective-permute-done((bf16[512,768]{1,0:T(8,128)(2,1)}, bf16[512,768]{1,0:T(8,128)(2,1)}, u32[]{:S(2)}, u32[]{:S(2)}) %collective-permute-start.2) | collective-permute-done | bytes 786464 | tf_op jit(solution)/shard_map/ppermute | solution.py:1094
  27.5 1.8 collective-permute-start.7
  30.0 3.7 %pairs.1 = (bf16[2,512,384]{2,1,0:T(8,128)(2,1)S(1)}, bf16[2,528,384]{2,1,0:T(8,128)(2,1)S(1)}, bf16[512,768]{1,0:T(8,128)(2,1)S(1)}, f32[8,768]{1,0:T(8,128)S(1)}, f32[1,3072]{1,0:T(1,128)S(1)}) custom-call(s32[5]{0:T(128)S(1)} %pad_add_fusion.refs_0_, bf16[512,768]{1,0:T(8,128)(2,1)S(1)} %copy-done.2, ...), custom_call_target="tpu_custom_call" | custom-call | flops 1 | bytes 1 | tf_op jit(solution)/shard_map/pairs/pallas_call | solution.py:120
  33.8 1.8 collective-permute-start.6
  37.1 1.6 queries.1
  38.7 10.3 %collective-permute-done.7.refs_0_ = bf16[272,1536]{1,0:T(8,128)(2,1)} collective-permute-done((bf16[272,1536]{1,0:T(8,128)(2,1)S(1)}, bf16[272,1536]{1,0:T(8,128)(2,1)}, u32[]{:S(2)}, u32[]{:S(2)}) %collective-permute-start.7) | collective-permute-done | bytes 835616 | tf_op jit(solution)/shard_map/ppermute | solution.py:1088
  49.0 1.8 collective-permute-start.9
  53.4 3.2 %attend.2 = (bf16[512,384]{1,0:T(8,128)(2,1)S(1)}, f32[3,4,256]{2,1,0:T(4,128)S(1)}) custom-call(bf16[512,768]{1,0:T(8,128)(2,1)S(1)} %get-tuple-element.158.refs_0_, bf16[2,512,384]{2,1,0:T(8,128)(2,1)S(1)} %get-tuple-element.159.refs_1_, bf16[2,512,384]{2,1,0:T(8,128)(2,1)S(1)} %collective-permute-done.6.refs_2_, ...), custom_call_target="tpu_custom_call" | custom-call | flops 60000002048 | bytes 62914560 | tf_op jit(solution)/shard_map/attend/pallas_call | solution.py:120
  56.7 12.8 %collective-permute-done.10.refs_0_ = bf16[192,2560]{1,0:T(8,128)(2,1)S(1)} collective-permute-done((bf16[192,2560]{1,0:T(8,128)(2,1)S(1)}, bf16[192,2560]{1,0:T(8,128)(2,1)S(1)}, u32[]{:S(2)}, u32[]{:S(2)}) %collective-permute-start.10) | collective-permute-done | bytes 983072 | tf_op jit(solution)/shard_map/ppermute | solution.py:1088
  71.1 3.2 %attend.3 = (bf16[512,384]{1,0:T(8,128)(2,1)S(1)}, f32[3,4,256]{2,1,0:T(4,128)S(1)}) custom-call(bf16[512,768]{1,0:T(8,128)(2,1)S(1)} %get-tuple-element.158.refs_0_, bf16[2,528,384]{2,1,0:T(8,128)(2,1)S(1)} %get-tuple-element.164.refs_1_, bf16[2,528,384]{2,1,0:T(8,128)(2,1)S(1)} %collective-permute-done.8.refs_2_.refs_6_.refs_5_, ...), custom_call_target="tpu_custom_call" | custom-call | flops 60000002048 | bytes 62914560 | tf_op jit(solution)/shard_map/attend/pallas_call | solution.py:120
  74.4 10.6 %middle.1 = (f32[512,768]{1,0:T(8,128)S(1)}, bf16[512,768]{1,0:T(8,128)(2,1)S(1)}, bf16[512,3072]{1,0:T(8,128)(2,1)S(1)}, bf16[512,3072]{1,0:T(8,128)(2,1)S(1)},...) custom-call(s32[5]{0:T(128)S(1)} %copy-done.28, ...), custom_call_target="tpu_custom_call" | custom-call | flops 1 | bytes 1 | tf_op jit(solution)/shard_map/middle/pallas_call | solution.py:120
  85.0 1.6 collective-permute-start.14
  86.6 2.2 collective-permute-done.14.refs_1_
  88.8 2.1 gate.1
  90.9 2.0 down_grads.2
  93.0 2.0 down_grads.3
  99.1 7.6 %chain.1 = (f32[512,768]{1,0:T(8,128)S(1)}, bf16[512,768]{1,0:T(8,128)(2,1)S(1)}, bf16[512,768]{1,0:T(8,128)(2,1)S(1)}, bf16[512,3072]{1,0:T(8,128)(2,1)S(1)}, f...) custom-call(s32[5]{0:T(128)S(1)} %copy-done.28, ...), custom_call_target="tpu_custom_call" | custom-call | flops 1 | bytes 1 | tf_op jit(solution)/shard_map/chain/pallas_call | solution.py:120
  106.7 5.4 %collective-permute-done.17.refs_2_ = bf16[192,1536]{1,0:T(8,128)(2,1)S(1)} collective-permute-done((bf16[192,1536]{1,0:T(8,128)(2,1)S(1)}, bf16[192,1536]{1,0:T(8,128)(2,1)S(1)}, u32[]{:S(2)}, u32[]{:S(2)}) %collective-permute-start.17) | collective-permute-done | bytes 589856 | tf_op jit(solution)/shard_map/ppermute | solution.py:1088
  114.4 3.5 %collective-permute-start.21 = (bf16[192,1536]{1,0:T(8,128)(2,1)S(1)}, bf16[192,1536]{1,0:T(8,128)(2,1)S(1)}, u32[]{:S(2)}, u32[]{:S(2)}) collective-permute-start(bf16[192,1536]{1,0:T(8,128)(2,1)S(1)} %get-tuple-element.207.refs_3_), channel_id=1, source_target_pairs={{0,1},{3,2},{4,5},{7,6},{8,9},{11,10},{12,13},{15,14},{16,17},{19,... | collective-permute-start | bytes 1769480 | tf_op jit(solution)/shard_map/ppermute | solution.py:1098
  118.3 3.4 %up_grads.1 = (bf16[2,192,1536]{2,1,0:T(8,128)(2,1)S(1)}, bf16[2,192,1536]{2,1,0:T(8,128)(2,1)S(1)}, bf16[2,192,1536]{2,1,0:T(8,128)(2,1)S(1)}, bf16[2,192,1536]{2,1,0:T(8,128)(2,1)S(1)}, f32[8,128]{1,0:T(8,128)S(1)}) custom-call(s32[5]{0:T(128)S(1)} %copy-done.28, bf16[512,768]{1,0:T(8,128)(2,1)S(1)} %get-tuple-element.190.refs_1_, ...), custom_call_target="tpu_custom_call" | custom-call | flops 1 | bytes 1 | tf_op jit(solution)/shard_map/up_grads/pallas_call | solution.py:120
  121.8 4.9 %attend_back.2 = (bf16[512,384]{1,0:T(8,128)(2,1)S(1)}, f32[2,512,384]{2,1,0:T(8,128)S(1)}, bf16[2,512,384]{2,1,0:T(8,128)(2,1)S(1)}, f32[8,128]{1,0:T(8,128)S(1)}) custom-call(bf16[512,768]{1,0:T(8,128)(2,1)S(1)} %copy-done.37, bf16[2,512,384]{2,1,0:T(8,128)(2,1)S(1)} %copy-done.39, bf16[2,512,384]{2,1,0:T(8,128)(2,1)S(1)} %copy-done.41, ...), custom_call_target="tpu_custom_call" | custom-call | flops 60000002048 | bytes 62914560 | tf_op jit(solution)/shard_map/attend_back/pallas_call | solution.py:120
  126.8 1.6 collective-permute-start.22
  130.4 4.4 %collective-permute-start.23 = (bf16[192,1536]{1,0:T(8,128)(2,1)S(1)}, bf16[192,1536]{1,0:T(8,128)(2,1)S(1)}, u32[]{:S(2)}, u32[]{:S(2)}) collective-permute-start(bf16[192,1536]{1,0:T(8,128)(2,1)S(1)} %get-tuple-element.216.refs_1_), channel_id=1, source_target_pairs={{0,1},{3,2},{4,5},{7,6},{8,9},{11,10},{12,13},{15,14},{16,17},{19,... | collective-permute-start | bytes 1769480 | tf_op jit(solution)/shard_map/ppermute | solution.py:1098
  138.3 5.0 %attend_back.3 = (bf16[512,384]{1,0:T(8,128)(2,1)S(1)}, f32[2,512,384]{2,1,0:T(8,128)S(1)}, bf16[2,528,384]{2,1,0:T(8,128)(2,1)S(1)}, f32[8,128]{1,0:T(8,128)S(1)}) custom-call(bf16[512,768]{1,0:T(8,128)(2,1)S(1)} %copy-done.37, bf16[2,528,384]{2,1,0:T(8,128)(2,1)S(1)} %copy-done.35, bf16[2,528,384]{2,1,0:T(8,128)(2,1)S(1)} %collective-permute-done.8.refs_2_.refs_6_.refs_5_, ...), custom_call_target="tpu_custom_call" | custom-call | flops 60000002048 | bytes 62914560 | tf_op jit(solution)/shard_map/attend_back/pallas_call | solution.py:120
  143.3 2.4 collective-permute-done.23.refs_2_
  145.7 4.3 %collective-permute-done.24.refs_4_ = bf16[192,1536]{1,0:T(8,128)(2,1)S(1)} collective-permute-done((bf16[192,1536]{1,0:T(8,128)(2,1)S(1)}, bf16[192,1536]{1,0:T(8,128)(2,1)S(1)}, u32[]{:S(2)}, u32[]{:S(2)}) %collective-permute-start.24) | collective-permute-done | bytes 589856 | tf_op jit(solution)/shard_map/ppermute | solution.py:1088
  151.5 2.2 collective-permute-start.27
  154.4 1.6 collective-permute-start.33
  156.0 3.5 %lead_grads.1 = (bf16[2,512,384]{2,1,0:T(8,128)(2,1)S(1)}, bf16[2,192,2304]{2,1,0:T(8,128)(2,1)S(1)}, bf16[2,192,2304]{2,1,0:T(8,128)(2,1)S(1)}, f32[8,128]{1,0:T(8,128)S(1)}) custom-call(s32[5]{0:T(128)S(1)} %copy-done.28, bf16[512,384]{1,0:T(8,128)(2,1)S(1)} %copy-done.15, bf16[512,384]{1,0:T(8,128)(2,1)S(1)} %copy-done.17, ...), custom_call_target="tpu_custom_call" | custom-call | flops 1 | bytes 1 | tf_op jit(solution)/shard_map/lead_grads/pallas_call | solution.py:120
  159.6 3.6 %collective-permute-done.28.refs_4_ = bf16[192,1536]{1,0:T(8,128)(2,1)S(1)} collective-permute-done((bf16[192,1536]{1,0:T(8,128)(2,1)S(1)}, bf16[192,1536]{1,0:T(8,128)(2,1)S(1)}, u32[]{:S(2)}, u32[]{:S(2)}) %collective-permute-start.28) | collective-permute-done | bytes 589856 | tf_op jit(solution)/shard_map/ppermute | solution.py:1088
  164.8 3.7 %collective-permute-start.30 = (bf16[192,1536]{1,0:T(8,128)(2,1)S(1)}, bf16[192,1536]{1,0:T(8,128)(2,1)S(1)}, u32[]{:S(2)}, u32[]{:S(2)}) collective-permute-start(bf16[192,1536]{1,0:T(8,128)(2,1)S(1)} %get-tuple-element.232.refs_2_), channel_id=1, source_target_pairs={{0,1},{1,0},{2,3},{3,2},{4,5},{5,4},{6,7},{7,6},{8,9},{9,8},{10,11... | collective-permute-start | bytes 1769480 | tf_op jit(solution)/shard_map/ppermute | solution.py:1098
  172.0 6.0 %first.1 = (f32[512,768]{1,0:T(8,128)}, bf16[400,768]{1,0:T(8,128)(2,1)S(1)}, bf16[400,768]{1,0:T(8,128)(2,1)S(1)}, f32[8,128]{1,0:T(8,128)S(1)}) custom-call(s32[5]{0:T(128)S(1)} %copy-done.28, f32[512,768]{1,0:T(8,128)S(1)} %get-tuple-element.236.refs_1_, bf16[512,768]{1,0:T(8,128)(2,1)S(1)} %copy-done.4, f32[8,768]{1,0:T(8,128)S(1)} %copy-done.25, ...), custom_call_target="tpu_custom_call" | custom-call | flops 1 | bytes 1 | tf_op jit(solution)/shard_map/first/pallas_call | solution.py:120
  178.0 3.1 %collective-permute-done.31.refs_4_ = bf16[192,1536]{1,0:T(8,128)(2,1)S(1)} collective-permute-done((bf16[192,1536]{1,0:T(8,128)(2,1)S(1)}, bf16[192,1536]{1,0:T(8,128)(2,1)S(1)}, u32[]{:S(2)}, u32[]{:S(2)}) %collective-permute-start.31) | collective-permute-done | bytes 589856 | tf_op jit(solution)/shard_map/ppermute | solution.py:1088
  183.7 2.1 collective-permute-start.34
  187.8 2.6 %settle.3 = (f32[768,768]{1,0:T(8,128)}, f32[8,128]{1,0:T(8,128)S(1)}) custom-call(s32[5]{0:T(128)S(1)} %copy-done.28, bf16[192,1536]{1,0:T(8,128)(2,1)S(1)} %get-tuple-element.225.refs_1_, bf16[192,1536]{1,0:T(8,128)(2,1)S(1)} %get-tuple-element.232.refs_2_, bf16[192,1536]{1,0:T(8,128)(2,1)S(1)} %collective-permute-done.27.refs_2_.refs_3_, ...), custom_call_target="tpu_custom_call" | custom-call | flops 1 | bytes 1 | tf_op jit(solution)/shard_map/settle/pallas_call | solution.py:120
  191.8 4.0 %collective-permute-done.34.refs_2_.refs_3_ = bf16[192,1536]{1,0:T(8,128)(2,1)S(1)} collective-permute-done((bf16[192,1536]{1,0:T(8,128)(2,1)S(1)}, bf16[192,1536]{1,0:T(8,128)(2,1)S(1)}, u32[]{:S(2)}, u32[]{:S(2)}) %collective-permute-start.34) | collective-permute-done | bytes 589856 | tf_op jit(solution)/shard_map/ppermute | solution.py:1098
  198.7 7.6 %collective-permute-start.38 = (bf16[192,768]{1,0:T(8,128)(2,1)S(1)}, bf16[192,768]{1,0:T(8,128)(2,1)S(1)}, u32[]{:S(2)}, u32[]{:S(2)}) collective-permute-start(bf16[192,768]{1,0:T(8,128)(2,1)S(1)} %get-tuple-element.253.refs_1_), channel_id=1, source_target_pairs={{0,1},{3,2},{4,5},{7,6},{8,9},{11,10},{12,13},{15,14},{16,17},{19,... | collective-permute-start | bytes 884744 | tf_op jit(solution)/shard_map/ppermute | solution.py:1098
  208.2 2.8 %collective-permute-done.38.refs_2_ = bf16[192,768]{1,0:T(8,128)(2,1)S(1)} collective-permute-done((bf16[192,768]{1,0:T(8,128)(2,1)S(1)}, bf16[192,768]{1,0:T(8,128)(2,1)S(1)}, u32[]{:S(2)}, u32[]{:S(2)}) %collective-permute-start.38) | collective-permute-done | bytes 294944 | tf_op jit(solution)/shard_map/ppermute | solution.py:1098
  211.7 1.6 collective-permute-start.40
  218.0 2.2 settle.4
  224.8 2.3 collective-permute-done.46.refs_4_.refs_3_
  228.2 9.6 %collective-permute-done.48.refs_4_ = bf16[192,768]{1,0:T(8,128)(2,1)S(1)} collective-permute-done((bf16[192,768]{1,0:T(8,128)(2,1)S(1)}, bf16[192,768]{1,0:T(8,128)(2,1)S(1)}, u32[]{:S(2)}, u32[]{:S(2)}) %collective-permute-start.48) | collective-permute-done | bytes 294944 | tf_op jit(solution)/shard_map/ppermute | solution.py:1098
  237.9 2.1 settle.5
  241.3 2.0 last_settle.1
  (193 shorter events, 54.5 us)
Async XLA Ops:
  3.1 24.2 %collective-permute-start.1 = (bf16[208,2304]{1,0:T(8,128)(2,1)S(1)}, bf16[208,2304]{1,0:T(8,128)(2,1)S(1)}, u32[]{:S(2)}, u32[]{:S(2)}) collective-permute-start(bf16[208,2304]{1,0:T(8,128)(2,1)S(1)} %get-tuple-element.151.refs_2_.refs_7_), channel_id=1, source_target_pairs={{0,8},{4,12},{8,0},{12,4},{16,24},{20,28},{24,16},{28,20},{1,9},{5... | collective-permute-start | bytes 2875400 | tf_op jit(solution)/shard_map/ppermute | solution.py:1088
  6.1 21.2 %collective-permute-start = (bf16[208,2304]{1,0:T(8,128)(2,1)S(1)}, bf16[208,2304]{1,0:T(8,128)(2,1)S(1)}, u32[]{:S(2)}, u32[]{:S(2)}) collective-permute-start(bf16[208,2304]{1,0:T(8,128)(2,1)S(1)} %get-tuple-element.151.refs_2_.refs_7_), channel_id=1, source_target_pairs={{0,4},{4,0},{8,12},{12,8},{16,20},{20,16},{24,28},{28,24},{1,5},{5... | collective-permute-start | bytes 2875400 | tf_op jit(solution)/shard_map/ppermute | solution.py:1088
  6.1 20.3 %collective-permute-start.2 = (bf16[512,768]{1,0:T(8,128)(2,1)}, bf16[512,768]{1,0:T(8,128)(2,1)}, u32[]{:S(2)}, u32[]{:S(2)}) collective-permute-start(bf16[512,768]{1,0:T(8,128)(2,1)} %refs_2_.4), channel_id=1, source_target_pairs={{0,16},{4,20},{8,24},{12,28},{16,0},{20,4},{24,8},{28,12},{1,17},{... | collective-permute-start | bytes 2359304 | tf_op jit(solution)/shard_map/ppermute | solution.py:1094
  12.9 16.4 %collective-permute-start.4 = (bf16[192,3840]{1,0:T(8,128)(2,1)S(1)}, bf16[192,3840]{1,0:T(8,128)(2,1)S(1)}, u32[]{:S(2)}, u32[]{:S(2)}) collective-permute-start(bf16[192,3840]{1,0:T(8,128)(2,1)S(1)} %get-tuple-element.154.refs_8_), channel_id=1, source_target_pairs={{0,4},{4,0},{8,12},{12,8},{16,20},{20,16},{24,28},{28,24},{1,5},{5... | collective-permute-start | bytes 4423688 | tf_op jit(solution)/shard_map/ppermute | solution.py:1088
  13.2 16.1 %collective-permute-start.5 = (bf16[768,768]{1,0:T(8,128)(2,1)S(1)}, bf16[768,768]{1,0:T(8,128)(2,1)S(1)}, u32[]{:S(2)}, u32[]{:S(2)}) collective-permute-start(bf16[768,768]{1,0:T(8,128)(2,1)S(1)} %get-tuple-element.155.refs_10_), channel_id=1, source_target_pairs={{0,4},{4,0},{8,12},{12,8},{16,20},{20,16},{24,28},{28,24},{1,5},{5... | collective-permute-start | bytes 3538952 | tf_op jit(solution)/shard_map/ppermute | solution.py:1088
  27.5 21.6 %collective-permute-start.7 = (bf16[272,1536]{1,0:T(8,128)(2,1)S(1)}, bf16[272,1536]{1,0:T(8,128)(2,1)}, u32[]{:S(2)}, u32[]{:S(2)}) collective-permute-start(bf16[272,1536]{1,0:T(8,128)(2,1)S(1)} %get-tuple-element.161), channel_id=1, source_target_pairs={{0,8},{4,12},{8,0},{12,4},{16,24},{20,28},{24,16},{28,20},{1,9},{5... | collective-permute-start | bytes 2506760 | tf_op jit(solution)/shard_map/ppermute | solution.py:1088
  33.8 19.7 %collective-permute-start.6 = (bf16[2,512,384]{2,1,0:T(8,128)(2,1)S(1)}, bf16[2,512,384]{2,1,0:T(8,128)(2,1)S(1)}, u32[]{:S(2)}, u32[]{:S(2)}) collective-permute-start(bf16[2,512,384]{2,1,0:T(8,128)(2,1)S(1)} %get-tuple-element.159.refs_1_), channel_id=1, source_target_pairs={{0,16},{4,20},{8,24},{12,28},{16,0},{20,4},{24,8},{28,12},{1,17},{... | collective-permute-start | bytes 2359304 | tf_op jit(solution)/shard_map/ppermute | solution.py:1094
  35.6 33.9 %collective-permute-start.10 = (bf16[192,2560]{1,0:T(8,128)(2,1)S(1)}, bf16[192,2560]{1,0:T(8,128)(2,1)S(1)}, u32[]{:S(2)}, u32[]{:S(2)}) collective-permute-start(bf16[192,2560]{1,0:T(8,128)(2,1)S(1)} %get-tuple-element.166), channel_id=1, source_target_pairs={{0,8},{4,12},{8,0},{12,4},{16,24},{20,28},{24,16},{28,20},{1,9},{5... | collective-permute-start | bytes 2949128 | tf_op jit(solution)/shard_map/ppermute | solution.py:1088
  49.0 25.3 %collective-permute-start.12 = (bf16[272,1536]{1,0:T(8,128)(2,1)}, bf16[272,1536]{1,0:T(8,128)(2,1)}, u32[]{:S(2)}, u32[]{:S(2)}) collective-permute-start(bf16[272,1536]{1,0:T(8,128)(2,1)} %hold.9.refs_5_.refs_14_), channel_id=1, source_target_pairs={{0,4},{4,0},{8,12},{12,8},{16,20},{20,16},{24,28},{28,24},{1,5},{5... | collective-permute-start | bytes 2506760 | tf_op jit(solution)/shard_map/ppermute | solution.py:1088
  49.0 21.3 %collective-permute-start.9 = (bf16[272,1536]{1,0:T(8,128)(2,1)}, bf16[272,1536]{1,0:T(8,128)(2,1)S(1)}, u32[]{:S(2)}, u32[]{:S(2)}) collective-permute-start(bf16[272,1536]{1,0:T(8,128)(2,1)} %hold.9.refs_5_.refs_14_), channel_id=1, source_target_pairs={{0,1},{1,0},{2,3},{3,2},{4,5},{5,4},{6,7},{7,6},{8,9},{9,8},{10,11... | collective-permute-start | bytes 2506760 | tf_op jit(solution)/shard_map/ppermute | solution.py:1098
  50.9 20.2 %collective-permute-start.8 = (bf16[2,528,384]{2,1,0:T(8,128)(2,1)S(1)}, bf16[2,528,384]{2,1,0:T(8,128)(2,1)S(1)}, u32[]{:S(2)}, u32[]{:S(2)}) collective-permute-start(bf16[2,528,384]{2,1,0:T(8,128)(2,1)S(1)} %get-tuple-element.164.refs_1_), channel_id=1, source_target_pairs={{0,16},{4,20},{8,24},{12,28},{16,0},{20,4},{24,8},{28,12},{1,17},{... | collective-permute-start | bytes 2433032 | tf_op jit(solution)/shard_map/ppermute | solution.py:1094
  69.5 4.8 %collective-permute-start.11 = (bf16[192,2560]{1,0:T(8,128)(2,1)S(1)}, bf16[192,2560]{1,0:T(8,128)(2,1)S(1)}, u32[]{:S(2)}, u32[]{:S(2)}) collective-permute-start(bf16[192,2560]{1,0:T(8,128)(2,1)S(1)} %hold.10.refs_1_.refs_12_), channel_id=1, source_target_pairs={{0,4},{4,0},{8,12},{12,8},{16,20},{20,16},{24,28},{28,24},{1,5},{5... | collective-permute-start | bytes 2949128 | tf_op jit(solution)/shard_map/ppermute | solution.py:1088
  70.4 3.9 %collective-permute-start.13 = (bf16[272,1536]{1,0:T(8,128)(2,1)S(1)}, bf16[272,1536]{1,0:T(8,128)(2,1)S(1)}, u32[]{:S(2)}, u32[]{:S(2)}) collective-permute-start(bf16[272,1536]{1,0:T(8,128)(2,1)S(1)} %hold.11.refs_5_.refs_15_), channel_id=1, source_target_pairs={{0,4},{4,0},{8,12},{12,8},{16,20},{20,16},{24,28},{28,24},{1,5},{5... | collective-permute-start | bytes 2506760 | tf_op jit(solution)/shard_map/ppermute | solution.py:1088
  85.0 3.8 %collective-permute-start.14 = (f32[8,512]{1,0:T(8,128)S(1)}, f32[8,512]{1,0:T(8,128)S(1)}, u32[]{:S(2)}, u32[]{:S(2)}) collective-permute-start(f32[8,512]{1,0:T(8,128)S(1)} %get-tuple-element.171.refs_0_.refs_6_), channel_id=1, source_target_pairs={{0,16},{4,20},{8,24},{12,28},{16,0},{20,4},{24,8},{28,12},{1,17},{... | collective-permute-start | bytes 49160 | tf_op jit(solution)/shard_map/ppermute | solution.py:1094
  93.0 2.9 %collective-permute-start.16 = (bf16[2,192,1536]{2,1,0:T(8,128)(2,1)S(1)}, bf16[2,192,1536]{2,1,0:T(8,128)(2,1)S(1)}, u32[]{:S(2)}, u32[]{:S(2)}) collective-permute-start(bf16[2,192,1536]{2,1,0:T(8,128)(2,1)S(1)} %get-tuple-element.184), channel_id=1, source_target_pairs={{0,4},{4,0},{8,12},{12,8},{16,20},{20,16},{24,28},{28,24},{1,5},{5... | collective-permute-start | bytes 3538952 | tf_op jit(solution)/shard_map/ppermute | solution.py:1088
  95.0 3.2 %collective-permute-start.15 = (bf16[2,192,1536]{2,1,0:T(8,128)(2,1)S(1)}, bf16[2,192,1536]{2,1,0:T(8,128)(2,1)S(1)}, u32[]{:S(2)}, u32[]{:S(2)}) collective-permute-start(bf16[2,192,1536]{2,1,0:T(8,128)(2,1)S(1)} %get-tuple-element.182), channel_id=1, source_target_pairs={{0,4},{4,0},{8,12},{12,8},{16,20},{20,16},{24,28},{28,24},{1,5},{5... | collective-permute-start | bytes 3538952 | tf_op jit(solution)/shard_map/ppermute | solution.py:1088
  96.7 15.4 %collective-permute-start.17 = (bf16[192,1536]{1,0:T(8,128)(2,1)S(1)}, bf16[192,1536]{1,0:T(8,128)(2,1)S(1)}, u32[]{:S(2)}, u32[]{:S(2)}) collective-permute-start(bf16[192,1536]{1,0:T(8,128)(2,1)S(1)} %get-tuple-element.195), channel_id=1, source_target_pairs={{0,8},{4,12},{8,0},{12,4},{16,24},{20,28},{24,16},{28,20},{1,9},{5... | collective-permute-start | bytes 1769480 | tf_op jit(solution)/shard_map/ppermute | solution.py:1088
  112.8 16.0 %collective-permute-start.20 = (bf16[192,1536]{1,0:T(8,128)(2,1)S(1)}, bf16[192,1536]{1,0:T(8,128)(2,1)S(1)}, u32[]{:S(2)}, u32[]{:S(2)}) collective-permute-start(bf16[192,1536]{1,0:T(8,128)(2,1)S(1)} %hold.12.refs_2_), channel_id=1, source_target_pairs={{0,8},{4,12},{8,0},{12,4},{16,24},{20,28},{24,16},{28,20},{1,9},{5... | collective-permute-start | bytes 1769480 | tf_op jit(solution)/shard_map/ppermute | solution.py:1088
  114.4 15.2 %collective-permute-start.21 = (bf16[192,1536]{1,0:T(8,128)(2,1)S(1)}, bf16[192,1536]{1,0:T(8,128)(2,1)S(1)}, u32[]{:S(2)}, u32[]{:S(2)}) collective-permute-start(bf16[192,1536]{1,0:T(8,128)(2,1)S(1)} %get-tuple-element.207.refs_3_), channel_id=1, source_target_pairs={{0,1},{3,2},{4,5},{7,6},{8,9},{11,10},{12,13},{15,14},{16,17},{19,... | collective-permute-start | bytes 1769480 | tf_op jit(solution)/shard_map/ppermute | solution.py:1098
  126.8 29.3 %collective-permute-start.22 = (bf16[2,512,384]{2,1,0:T(8,128)(2,1)S(1)}, bf16[2,512,384]{2,1,0:T(8,128)(2,1)S(1)}, u32[]{:S(2)}, u32[]{:S(2)}) collective-permute-start(bf16[2,512,384]{2,1,0:T(8,128)(2,1)S(1)} %get-tuple-element.214), channel_id=1, source_target_pairs={{0,16},{4,20},{8,24},{12,28},{16,0},{20,4},{24,8},{28,12},{1,17},{... | collective-permute-start | bytes 2359304 | tf_op jit(solution)/shard_map/ppermute | solution.py:1094
  128.3 9.1 %collective-permute-start.18 = (bf16[2,192,1536]{2,1,0:T(8,128)(2,1)S(1)}, bf16[2,192,1536]{2,1,0:T(8,128)(2,1)S(1)}, u32[]{:S(2)}, u32[]{:S(2)}) collective-permute-start(bf16[2,192,1536]{2,1,0:T(8,128)(2,1)S(1)} %get-tuple-element.203), channel_id=1, source_target_pairs={{0,4},{4,0},{8,12},{12,8},{16,20},{20,16},{24,28},{28,24},{1,5},{5... | collective-permute-start | bytes 3538952 | tf_op jit(solution)/shard_map/ppermute | solution.py:1088
  128.3 7.6 %collective-permute-start.19 = (bf16[2,192,1536]{2,1,0:T(8,128)(2,1)S(1)}, bf16[2,192,1536]{2,1,0:T(8,128)(2,1)S(1)}, u32[]{:S(2)}, u32[]{:S(2)}) collective-permute-start(bf16[2,192,1536]{2,1,0:T(8,128)(2,1)S(1)} %get-tuple-element.205), channel_id=1, source_target_pairs={{0,4},{4,0},{8,12},{12,8},{16,20},{20,16},{24,28},{28,24},{1,5},{5... | collective-permute-start | bytes 3538952 | tf_op jit(solution)/shard_map/ppermute | solution.py:1088
  130.4 15.2 %collective-permute-start.23 = (bf16[192,1536]{1,0:T(8,128)(2,1)S(1)}, bf16[192,1536]{1,0:T(8,128)(2,1)S(1)}, u32[]{:S(2)}, u32[]{:S(2)}) collective-permute-start(bf16[192,1536]{1,0:T(8,128)(2,1)S(1)} %get-tuple-element.216.refs_1_), channel_id=1, source_target_pairs={{0,1},{3,2},{4,5},{7,6},{8,9},{11,10},{12,13},{15,14},{16,17},{19,... | collective-permute-start | bytes 1769480 | tf_op jit(solution)/shard_map/ppermute | solution.py:1098
  134.9 10.8 %collective-permute-start.25 = (bf16[192,1536]{1,0:T(8,128)(2,1)S(1)}, bf16[192,1536]{1,0:T(8,128)(2,1)S(1)}, u32[]{:S(2)}, u32[]{:S(2)}) collective-permute-start(bf16[192,1536]{1,0:T(8,128)(2,1)S(1)} %get-tuple-element.219.refs_5_), channel_id=1, source_target_pairs={{1,2},{2,1},{5,6},{6,5},{9,10},{10,9},{13,14},{14,13},{17,18},{18,... | collective-permute-start | bytes 1769480 | tf_op jit(solution)/shard_map/ppermute | solution.py:1098
  136.8 13.1 %collective-permute-start.24 = (bf16[192,1536]{1,0:T(8,128)(2,1)S(1)}, bf16[192,1536]{1,0:T(8,128)(2,1)S(1)}, u32[]{:S(2)}, u32[]{:S(2)}) collective-permute-start(bf16[192,1536]{1,0:T(8,128)(2,1)S(1)} %get-tuple-element.218), channel_id=1, source_target_pairs={{0,8},{4,12},{8,0},{12,4},{16,24},{20,28},{24,16},{28,20},{1,9},{5... | collective-permute-start | bytes 1769480 | tf_op jit(solution)/shard_map/ppermute | solution.py:1088
  151.0 12.2 %collective-permute-start.28 = (bf16[192,1536]{1,0:T(8,128)(2,1)S(1)}, bf16[192,1536]{1,0:T(8,128)(2,1)S(1)}, u32[]{:S(2)}, u32[]{:S(2)}) collective-permute-start(bf16[192,1536]{1,0:T(8,128)(2,1)S(1)} %hold.13.refs_9_), channel_id=1, source_target_pairs={{0,8},{4,12},{8,0},{12,4},{16,24},{20,28},{24,16},{28,20},{1,9},{5... | collective-permute-start | bytes 1769480 | tf_op jit(solution)/shard_map/ppermute | solution.py:1088
  151.5 12.3 %collective-permute-start.27 = (bf16[192,1536]{1,0:T(8,128)(2,1)S(1)}, bf16[192,1536]{1,0:T(8,128)(2,1)S(1)}, u32[]{:S(2)}, u32[]{:S(2)}) collective-permute-start(bf16[192,1536]{1,0:T(8,128)(2,1)S(1)} %get-tuple-element.225.refs_1_), channel_id=1, source_target_pairs={{0,1},{1,0},{2,3},{3,2},{4,5},{5,4},{6,7},{7,6},{8,9},{9,8},{10,11... | collective-permute-start | bytes 1769480 | tf_op jit(solution)/shard_map/ppermute | solution.py:1098
  153.7 10.1 %collective-permute-start.29 = (bf16[192,1536]{1,0:T(8,128)(2,1)S(1)}, bf16[192,1536]{1,0:T(8,128)(2,1)S(1)}, u32[]{:S(2)}, u32[]{:S(2)}) collective-permute-start(bf16[192,1536]{1,0:T(8,128)(2,1)S(1)} %get-tuple-element.227.refs_5_), channel_id=1, source_target_pairs={{1,2},{2,1},{5,6},{6,5},{9,10},{10,9},{13,14},{14,13},{17,18},{18,... | collective-permute-start | bytes 1769480 | tf_op jit(solution)/shard_map/ppermute | solution.py:1098
  154.4 17.5 %collective-permute-start.33 = (bf16[2,528,384]{2,1,0:T(8,128)(2,1)S(1)}, bf16[2,528,384]{2,1,0:T(8,128)(2,1)S(1)}, u32[]{:S(2)}, u32[]{:S(2)}) collective-permute-start(bf16[2,528,384]{2,1,0:T(8,128)(2,1)S(1)} %get-tuple-element.238), channel_id=1, source_target_pairs={{0,16},{4,20},{8,24},{12,28},{16,0},{20,4},{24,8},{28,12},{1,17},{... | collective-permute-start | bytes 2433032 | tf_op jit(solution)/shard_map/ppermute | solution.py:1094
  159.5 9.9 %collective-permute-start.26 = (bf16[2,192,2304]{2,1,0:T(8,128)(2,1)S(1)}, bf16[2,192,2304]{2,1,0:T(8,128)(2,1)S(1)}, u32[]{:S(2)}, u32[]{:S(2)}) collective-permute-start(bf16[2,192,2304]{2,1,0:T(8,128)(2,1)S(1)} %get-tuple-element.223), channel_id=1, source_target_pairs={{0,4},{4,0},{8,12},{12,8},{16,20},{20,16},{24,28},{28,24},{1,5},{5... | collective-permute-start | bytes 5308424 | tf_op jit(solution)/shard_map/ppermute | solution.py:1088
  164.8 13.2 %collective-permute-start.30 = (bf16[192,1536]{1,0:T(8,128)(2,1)S(1)}, bf16[192,1536]{1,0:T(8,128)(2,1)S(1)}, u32[]{:S(2)}, u32[]{:S(2)}) collective-permute-start(bf16[192,1536]{1,0:T(8,128)(2,1)S(1)} %get-tuple-element.232.refs_2_), channel_id=1, source_target_pairs={{0,1},{1,0},{2,3},{3,2},{4,5},{5,4},{6,7},{7,6},{8,9},{9,8},{10,11... | collective-permute-start | bytes 1769480 | tf_op jit(solution)/shard_map/ppermute | solution.py:1098
  168.5 9.5 %collective-permute-start.32 = (bf16[192,1536]{1,0:T(8,128)(2,1)S(1)}, bf16[192,1536]{1,0:T(8,128)(2,1)S(1)}, u32[]{:S(2)}, u32[]{:S(2)}) collective-permute-start(bf16[192,1536]{1,0:T(8,128)(2,1)S(1)} %get-tuple-element.235.refs_5_), channel_id=1, source_target_pairs={{1,2},{2,1},{5,6},{6,5},{9,10},{10,9},{13,14},{14,13},{17,18},{18,... | collective-permute-start | bytes 1769480 | tf_op jit(solution)/shard_map/ppermute | solution.py:1098
  170.4 10.7 %collective-permute-start.31 = (bf16[192,1536]{1,0:T(8,128)(2,1)S(1)}, bf16[192,1536]{1,0:T(8,128)(2,1)S(1)}, u32[]{:S(2)}, u32[]{:S(2)}) collective-permute-start(bf16[192,1536]{1,0:T(8,128)(2,1)S(1)} %get-tuple-element.234), channel_id=1, source_target_pairs={{0,8},{4,12},{8,0},{12,4},{16,24},{20,28},{24,16},{28,20},{1,9},{5... | collective-permute-start | bytes 1769480 | tf_op jit(solution)/shard_map/ppermute | solution.py:1088
  178.0 8.5 %collective-permute-start.37 = (bf16[400,768]{1,0:T(8,128)(2,1)S(1)}, bf16[400,768]{1,0:T(8,128)(2,1)S(1)}, u32[]{:S(2)}, u32[]{:S(2)}) collective-permute-start(bf16[400,768]{1,0:T(8,128)(2,1)S(1)} %get-tuple-element.250), channel_id=1, source_target_pairs={{0,4},{4,0},{8,12},{12,8},{16,20},{20,16},{24,28},{28,24},{1,5},{5... | collective-permute-start | bytes 1843208 | tf_op jit(solution)/shard_map/ppermute | solution.py:1088
  182.1 9.6 %collective-permute-start.36 = (bf16[192,768]{1,0:T(8,128)(2,1)S(1)}, bf16[192,768]{1,0:T(8,128)(2,1)S(1)}, u32[]{:S(2)}, u32[]{:S(2)}) collective-permute-start(bf16[192,768]{1,0:T(8,128)(2,1)S(1)} %hold.14.refs_1_), channel_id=1, source_target_pairs={{0,8},{4,12},{8,0},{12,4},{16,24},{20,28},{24,16},{28,20},{1,9},{5... | collective-permute-start | bytes 884744 | tf_op jit(solution)/shard_map/ppermute | solution.py:1088
  183.7 12.1 %collective-permute-start.34 = (bf16[192,1536]{1,0:T(8,128)(2,1)S(1)}, bf16[192,1536]{1,0:T(8,128)(2,1)S(1)}, u32[]{:S(2)}, u32[]{:S(2)}) collective-permute-start(bf16[192,1536]{1,0:T(8,128)(2,1)S(1)} %get-tuple-element.246.refs_1_), channel_id=1, source_target_pairs={{0,1},{1,0},{2,3},{3,2},{4,5},{5,4},{6,7},{7,6},{8,9},{9,8},{10,11... | collective-permute-start | bytes 1769480 | tf_op jit(solution)/shard_map/ppermute | solution.py:1098
  185.8 9.9 %collective-permute-start.35 = (bf16[192,1536]{1,0:T(8,128)(2,1)S(1)}, bf16[192,1536]{1,0:T(8,128)(2,1)S(1)}, u32[]{:S(2)}, u32[]{:S(2)}) collective-permute-start(bf16[192,1536]{1,0:T(8,128)(2,1)S(1)} %get-tuple-element.247.refs_3_), channel_id=1, source_target_pairs={{1,2},{2,1},{5,6},{6,5},{9,10},{10,9},{13,14},{14,13},{17,18},{18,... | collective-permute-start | bytes 1769480 | tf_op jit(solution)/shard_map/ppermute | solution.py:1098
  187.2 19.1 %collective-permute-start.39 = (bf16[208,768]{1,0:T(8,128)(2,1)S(1)}, bf16[208,768]{1,0:T(8,128)(2,1)S(1)}, u32[]{:S(2)}, u32[]{:S(2)}) collective-permute-start(bf16[208,768]{1,0:T(8,128)(2,1)S(1)} %get-tuple-element.255), channel_id=1, source_target_pairs={{0,8},{4,12},{8,0},{12,4},{16,24},{20,28},{24,16},{28,20},{1,9},{5... | collective-permute-start | bytes 958472 | tf_op jit(solution)/shard_map/ppermute | solution.py:1088
  196.6 17.9 %collective-permute-start.41 = (bf16[192,1536]{1,0:T(8,128)(2,1)S(1)}, bf16[192,1536]{1,0:T(8,128)(2,1)S(1)}, u32[]{:S(2)}, u32[]{:S(2)}) collective-permute-start(bf16[192,1536]{1,0:T(8,128)(2,1)S(1)} %get-tuple-element.259.refs_1_), channel_id=1, source_target_pairs={{1,2},{2,1},{5,6},{6,5},{9,10},{10,9},{13,14},{14,13},{17,18},{18,... | collective-permute-start | bytes 1769480 | tf_op jit(solution)/shard_map/ppermute | solution.py:1098
  197.4 17.2 %collective-permute-start.43 = (bf16[192,1536]{1,0:T(8,128)(2,1)S(1)}, bf16[192,1536]{1,0:T(8,128)(2,1)S(1)}, u32[]{:S(2)}, u32[]{:S(2)}) collective-permute-start(bf16[192,1536]{1,0:T(8,128)(2,1)S(1)} %get-tuple-element.261.refs_2_), channel_id=1, source_target_pairs={{1,0},{2,3},{5,4},{6,7},{9,8},{10,11},{13,12},{14,15},{17,16},{18,... | collective-permute-start | bytes 1769480 | tf_op jit(solution)/shard_map/ppermute | solution.py:1098
  198.7 12.4 %collective-permute-start.38 = (bf16[192,768]{1,0:T(8,128)(2,1)S(1)}, bf16[192,768]{1,0:T(8,128)(2,1)S(1)}, u32[]{:S(2)}, u32[]{:S(2)}) collective-permute-start(bf16[192,768]{1,0:T(8,128)(2,1)S(1)} %get-tuple-element.253.refs_1_), channel_id=1, source_target_pairs={{0,1},{3,2},{4,5},{7,6},{8,9},{11,10},{12,13},{15,14},{16,17},{19,... | collective-permute-start | bytes 884744 | tf_op jit(solution)/shard_map/ppermute | solution.py:1098
  206.9 7.6 %collective-permute-start.42 = (bf16[208,768]{1,0:T(8,128)(2,1)S(1)}, bf16[208,768]{1,0:T(8,128)(2,1)S(1)}, u32[]{:S(2)}, u32[]{:S(2)}) collective-permute-start(bf16[208,768]{1,0:T(8,128)(2,1)S(1)} %get-tuple-element.260.refs_3_), channel_id=1, source_target_pairs={{0,1},{3,2},{4,5},{7,6},{8,9},{11,10},{12,13},{15,14},{16,17},{19,... | collective-permute-start | bytes 958472 | tf_op jit(solution)/shard_map/ppermute | solution.py:1098
  211.7 13.0 %collective-permute-start.40 = (bf16[512,768]{1,0:T(8,128)(2,1)S(1)}, bf16[512,768]{1,0:T(8,128)(2,1)S(1)}, u32[]{:S(2)}, u32[]{:S(2)}) collective-permute-start(bf16[512,768]{1,0:T(8,128)(2,1)S(1)} %hold.15.refs_5_.refs_0_), channel_id=1, source_target_pairs={{0,16},{4,20},{8,24},{12,28},{16,0},{20,4},{24,8},{28,12},{1,17},{... | collective-permute-start | bytes 2359304 | tf_op jit(solution)/shard_map/ppermute | solution.py:1094
  215.3 11.8 %collective-permute-start.46 = (bf16[192,1536]{1,0:T(8,128)(2,1)S(1)}, bf16[192,1536]{1,0:T(8,128)(2,1)S(1)}, u32[]{:S(2)}, u32[]{:S(2)}) collective-permute-start(bf16[192,1536]{1,0:T(8,128)(2,1)S(1)} %get-tuple-element.268.refs_1_), channel_id=1, source_target_pairs={{1,0},{2,3},{5,4},{6,7},{9,8},{10,11},{13,12},{14,15},{17,16},{18,... | collective-permute-start | bytes 1769480 | tf_op jit(solution)/shard_map/ppermute | solution.py:1098
  216.6 5.5 %collective-permute-start.44 = (bf16[208,768]{1,0:T(8,128)(2,1)S(1)}, bf16[208,768]{1,0:T(8,128)(2,1)S(1)}, u32[]{:S(2)}, u32[]{:S(2)}) collective-permute-start(bf16[208,768]{1,0:T(8,128)(2,1)S(1)} %get-tuple-element.262.refs_1_), channel_id=1, source_target_pairs={{1,2},{2,1},{5,6},{6,5},{9,10},{10,9},{13,14},{14,13},{17,18},{18,... | collective-permute-start | bytes 958472 | tf_op jit(solution)/shard_map/ppermute | solution.py:1098
  217.3 2.9 %collective-permute-start.45 = (bf16[192,768]{1,0:T(8,128)(2,1)S(1)}, bf16[192,768]{1,0:T(8,128)(2,1)S(1)}, u32[]{:S(2)}, u32[]{:S(2)}) collective-permute-start(bf16[192,768]{1,0:T(8,128)(2,1)S(1)} %get-tuple-element.263.refs_1_), channel_id=1, source_target_pairs={{1,2},{2,1},{5,6},{6,5},{9,10},{10,9},{13,14},{14,13},{17,18},{18,... | collective-permute-start | bytes 884744 | tf_op jit(solution)/shard_map/ppermute | solution.py:1098
  220.8 17.1 %collective-permute-start.48 = (bf16[192,768]{1,0:T(8,128)(2,1)S(1)}, bf16[192,768]{1,0:T(8,128)(2,1)S(1)}, u32[]{:S(2)}, u32[]{:S(2)}) collective-permute-start(bf16[192,768]{1,0:T(8,128)(2,1)S(1)} %get-tuple-element.272.refs_2_), channel_id=1, source_target_pairs={{1,0},{2,3},{5,4},{6,7},{9,8},{10,11},{13,12},{14,15},{17,16},{18,... | collective-permute-start | bytes 884744 | tf_op jit(solution)/shard_map/ppermute | solution.py:1098
  222.7 18.6 %collective-permute-start.47 = (bf16[208,768]{1,0:T(8,128)(2,1)S(1)}, bf16[208,768]{1,0:T(8,128)(2,1)S(1)}, u32[]{:S(2)}, u32[]{:S(2)}) collective-permute-start(bf16[208,768]{1,0:T(8,128)(2,1)S(1)} %get-tuple-element.271.refs_1_), channel_id=1, source_target_pairs={{1,0},{2,3},{5,4},{6,7},{9,8},{10,11},{13,12},{14,15},{17,16},{18,... | collective-permute-start | bytes 958472 | tf_op jit(solution)/shard_map/ppermute | solution.py:1098
  (45 other events, 405.8 us)
where the time goes:
time: 248 us; the launch traced here: 244 us
  waiting for transfers between devices  86.3 us (35%)
  Pallas kernels  84.8 us (34%)
  starting transfers between devices  64.7 us (26%)
  local copies, waits for them, and re-layouts  5.88 us (2%)
    pallas_call x51, Pallas kernels, call(): pl.pallas_call(wrapped, out_shape=outs, grid_spec=pltpu.PrefetchScalarGri...  84.8 us
    ppermute x23, waiting for transfers between devices, swap_bit(): lax.ppermute(value, axis, [(source, source ^ 1 << bit) for source in rang...  42.8 us
    ppermute x19, starting transfers between devices, along(): return lax.ppermute(value, 'dp', pairs)  37.2 us
    ppermute x19, waiting for transfers between devices, along(): return lax.ppermute(value, 'dp', pairs)  25.9 us
    ppermute x7, waiting for transfers between devices, from_partner(): lax.ppermute(value, 'stream', [(source, (source + half) % size) for sourc...  17.6 us
    ppermute x23, starting transfers between devices, swap_bit(): lax.ppermute(value, axis, [(source, source ^ 1 << bit) for source in rang...  16.2 us
    ppermute x7, starting transfers between devices, from_partner(): lax.ppermute(value, 'stream', [(source, (source + half) % size) for sourc...  11.2 us
    unnamed x88, local copies, waits for them, and re-layouts  4.99 us
  transfers between devices with their start and end apart: 49, of which 25 were waited for; matrix products, arithmetic and copies ran while one was open for 0% of the time, Pallas kernels for 28%

commit v1 on v0

--- a/solution.py
+++ b/solution.py
@@ -904,6 +904,34 @@
                 out[place, :, k * width : (k + 1) * width] = block[k * rows : (k + 1) * rows]
 
 
+def gate_lead_kernel(count, height, fold, places, hidden, *rest):
+    gate_kernel(*rest[:10])
+    down_grads_kernel(count, 0, height, fold, places, rest[7], hidden, *rest[10:])
+
+
+def gate_lead_pass(
+    order, places, hidden, own, other, tangent, partner_tangent, vectors, partner, height, fold, count
+):
+    near, far = slots_of(count)
+    dims = (height // fold, fold * (FF // count))
+    return order.call(
+        functools.partial(gate_lead_kernel, count, height, fold),
+        [places, hidden, own, other, tangent, partner_tangent, vectors, partner],
+        [in_smem] + [in_vmem] * 7,
+        [
+            shape_of((SEQ, D), f32),
+            shape_of((SEQ, D), bf16),
+            shape_of((SEQ, 128), f32),
+            shape_of((1, D), f32),
+            shape_of((len(near), *dims), bf16),
+            shape_of((len(far), *dims), bf16),
+        ],
+        [in_vmem] * 6,
+        limit=16,
+        name="gate_lead",
+    )
+
+
 def down_grads(order, places, low, hidden, first, height, fold, count):
     near, far = slots_of(count)
     width = FF // count
@@ -1254,9 +1282,14 @@
         halves,
     )
     inner_other = from_partner(inner_own)
-    modal_grad, modal_low, columns, output_bias_grad = gate_pass(
-        order, inner_own, inner_other, cotangent, partner_tangent, vectors, other_pairs[-1]
-    )
+    if paired:
+        modal_grad, modal_low, columns, output_bias_grad, d1, d1_far = gate_lead_pass(
+            order, places, hidden, inner_own, inner_other, cotangent, partner_tangent, vectors, other_pairs[-1], 384, 2, count
+        )
+    else:
+        modal_grad, modal_low, columns, output_bias_grad = gate_pass(
+            order, inner_own, inner_other, cotangent, partner_tangent, vectors, other_pairs[-1]
+        )
 
     def attend_back_group(group):
         query_grad, own_grad, other_grad = attend_back(
@@ -1301,8 +1334,7 @@
     query_grads, own_grads, returned = [], [], []
     back = (order, places, modal_low, modal_grad, slope, middle, vectors, wide, down)
     if paired:
-        d1, far = down_grads(order, places, modal_low, hidden, 0, 384, 2, count)
-        d1_core = core(far)
+        d1_core = core(d1_far)
         d2, far = down_grads(order, places, modal_low, hidden, 384, 384, 2, count)
         d2_core = core(far)
         d1, away = sums_pass(order, places, folds=[(d1, d1_core, [FF // 2])])

time: 248 us -> 248 us (level)
    unnamed x88 -> x70, local copies, waits for them, and re-layouts: 4.99 us -> 5.6 us
    pallas_call x51 -> x50, Pallas kernels: 84.8 us -> 84.4 us  [call(): pl.pallas_call(wrapped, out_shape=outs, grid_spec=pltpu.PrefetchScalarGri...]
where the time goes in v1:
time: 248 us; the launch traced here: 244 us
  waiting for transfers between devices  86.5 us (35%)
  Pallas kernels  84.4 us (34%)
  starting transfers between devices  64.7 us (26%)
  local copies, waits for them, and re-layouts  6.5 us (3%)
    pallas_call x50, Pallas kernels, call(): pl.pallas_call(wrapped, out_shape=outs, grid_spec=pltpu.PrefetchScalarGri...  84.4 us
    ppermute x23, waiting for transfers between devices, swap_bit(): lax.ppermute(value, axis, [(source, source ^ 1 << bit) for source in rang...  42.9 us
    ppermute x19, starting transfers between devices, along(): return lax.ppermute(value, 'dp', pairs)  37.2 us
    ppermute x19, waiting for transfers between devices, along(): return lax.ppermute(value, 'dp', pairs)  26 us
    ppermute x7, waiting for transfers between devices, from_partner(): lax.ppermute(value, 'stream', [(source, (source + half) % size) for sourc...  17.6 us
    ppermute x23, starting transfers between devices, swap_bit(): lax.ppermute(value, axis, [(source, source ^ 1 << bit) for source in rang...  16.2 us
    ppermute x7, starting transfers between devices, from_partner(): lax.ppermute(value, 'stream', [(source, (source + half) % size) for sourc...  11.2 us
    unnamed x70, local copies, waits for them, and re-layouts  5.6 us
  transfers between devices with their start and end apart: 49, of which 25 were waited for; matrix products, arithmetic and copies ran while one was open for 0% of the time, Pallas kernels for 28%

profile of v1, /device:TPU:0, one launch (start us, length us, event | category | flops | bytes accessed | tf_op | source)
XLA Modules:
  0.0 243.9 jit_solution(888416173784399071)
XLA Ops:
  3.1 3.0 %collective-permute-start.1 = (bf16[208,2304]{1,0:T(8,128)(2,1)S(1)}, bf16[208,2304]{1,0:T(8,128)(2,1)S(1)}, u32[]{:S(2)}, u32[]{:S(2)}) collective-permute-start(bf16[208,2304]{1,0:T(8,128)(2,1)S(1)} %get-tuple-element.150.refs_2_.refs_7_), channel_id=1, source_target_pairs={{0,8},{4,12},{8,0},{12,4},{16,24},{20,28},{24,16},{28,20},{1,9},{5... | collective-permute-start | bytes 2875400 | tf_op jit(solution)/shard_map/ppermute | solution.py:1116
  7.8 1.7 copy-done.11
  9.4 1.7 copy-done.12
  11.1 1.8 cast.1
  13.5 12.9 %collective-permute-done.2.refs_2_.refs_4_.refs_5_ = bf16[512,768]{1,0:T(8,128)(2,1)} collective-permute-done((bf16[512,768]{1,0:T(8,128)(2,1)}, bf16[512,768]{1,0:T(8,128)(2,1)}, u32[]{:S(2)}, u32[]{:S(2)}) %collective-permute-start.2) | collective-permute-done | bytes 786464 | tf_op jit(solution)/shard_map/ppermute | solution.py:1122
  27.5 1.8 collective-permute-start.7
  30.0 3.7 %pairs.1 = (bf16[2,512,384]{2,1,0:T(8,128)(2,1)S(1)}, bf16[2,528,384]{2,1,0:T(8,128)(2,1)S(1)}, bf16[512,768]{1,0:T(8,128)(2,1)S(1)}, f32[8,768]{1,0:T(8,128)S(1)}, f32[1,3072]{1,0:T(1,128)S(1)}) custom-call(s32[5]{0:T(128)S(1)} %pad_add_fusion.refs_0_, bf16[512,768]{1,0:T(8,128)(2,1)S(1)} %copy-done.2, ...), custom_call_target="tpu_custom_call" | custom-call | flops 1 | bytes 1 | tf_op jit(solution)/shard_map/pairs/pallas_call | solution.py:120
  33.7 1.8 collective-permute-start.6
  37.1 1.6 queries.1
  38.7 10.3 %collective-permute-done.7.refs_0_ = bf16[272,1536]{1,0:T(8,128)(2,1)} collective-permute-done((bf16[272,1536]{1,0:T(8,128)(2,1)S(1)}, bf16[272,1536]{1,0:T(8,128)(2,1)}, u32[]{:S(2)}, u32[]{:S(2)}) %collective-permute-start.7) | collective-permute-done | bytes 835616 | tf_op jit(solution)/shard_map/ppermute | solution.py:1116
  49.0 1.8 collective-permute-start.9
  53.4 3.2 %attend.2 = (bf16[512,384]{1,0:T(8,128)(2,1)S(1)}, f32[3,4,256]{2,1,0:T(4,128)S(1)}) custom-call(bf16[512,768]{1,0:T(8,128)(2,1)S(1)} %get-tuple-element.157.refs_0_, bf16[2,512,384]{2,1,0:T(8,128)(2,1)S(1)} %get-tuple-element.158.refs_1_, bf16[2,512,384]{2,1,0:T(8,128)(2,1)S(1)} %collective-permute-done.6.refs_2_, ...), custom_call_target="tpu_custom_call" | custom-call | flops 60000002048 | bytes 62914560 | tf_op jit(solution)/shard_map/attend/pallas_call | solution.py:120
  56.7 12.9 %collective-permute-done.10.refs_0_ = bf16[192,2560]{1,0:T(8,128)(2,1)S(1)} collective-permute-done((bf16[192,2560]{1,0:T(8,128)(2,1)S(1)}, bf16[192,2560]{1,0:T(8,128)(2,1)S(1)}, u32[]{:S(2)}, u32[]{:S(2)}) %collective-permute-start.10) | collective-permute-done | bytes 983072 | tf_op jit(solution)/shard_map/ppermute | solution.py:1116
  71.1 3.2 %attend.3 = (bf16[512,384]{1,0:T(8,128)(2,1)S(1)}, f32[3,4,256]{2,1,0:T(4,128)S(1)}) custom-call(bf16[512,768]{1,0:T(8,128)(2,1)S(1)} %get-tuple-element.157.refs_0_, bf16[2,528,384]{2,1,0:T(8,128)(2,1)S(1)} %get-tuple-element.163.refs_1_, bf16[2,528,384]{2,1,0:T(8,128)(2,1)S(1)} %collective-permute-done.8.refs_2_.refs_6_.refs_7_, ...), custom_call_target="tpu_custom_call" | custom-call | flops 60000002048 | bytes 62914560 | tf_op jit(solution)/shard_map/attend/pallas_call | solution.py:120
  74.4 10.5 %middle.1 = (f32[512,768]{1,0:T(8,128)S(1)}, bf16[512,768]{1,0:T(8,128)(2,1)S(1)}, bf16[512,3072]{1,0:T(8,128)(2,1)S(1)}, bf16[512,3072]{1,0:T(8,128)(2,1)S(1)},...) custom-call(s32[5]{0:T(128)S(1)} %pad_add_fusion.refs_0_, ...), custom_call_target="tpu_custom_call" | custom-call | flops 1 | bytes 1 | tf_op jit(solution)/shard_map/middle/pallas_call | solution.py:120
  86.5 2.2 collective-permute-done.14.refs_3_
  89.4 3.6 %gate_lead.1 = (f32[512,768]{1,0:T(8,128)S(1)}, bf16[512,768]{1,0:T(8,128)(2,1)S(1)}, f32[512,128]{1,0:T(8,128)S(1)}, f32[1,768]{1,0:T(1,128)S(1)}, bf16[2,192,1...) custom-call(s32[5]{0:T(128)S(1)} %copy-done.22, bf16[512,3072]{1,0:T(8,128)(2,1)S(1)} %get-tuple-element.170.refs_1_.refs_2_, ...), custom_call_target="tpu_custom_call" | custom-call | flops 1 | bytes 1 | tf_op jit(solution)/shard_map/gate_lead/pallas_call | solution.py:120
  93.1 2.0 down_grads.1
  99.1 7.4 %chain.1 = (f32[512,768]{1,0:T(8,128)S(1)}, bf16[512,768]{1,0:T(8,128)(2,1)S(1)}, bf16[512,768]{1,0:T(8,128)(2,1)S(1)}, bf16[512,3072]{1,0:T(8,128)(2,1)S(1)}, f...) custom-call(s32[5]{0:T(128)S(1)} %copy-done.23, ...), custom_call_target="tpu_custom_call" | custom-call | flops 1 | bytes 1 | tf_op jit(solution)/shard_map/chain/pallas_call | solution.py:120
  106.6 5.6 %collective-permute-done.17.refs_2_ = bf16[192,1536]{1,0:T(8,128)(2,1)S(1)} collective-permute-done((bf16[192,1536]{1,0:T(8,128)(2,1)S(1)}, bf16[192,1536]{1,0:T(8,128)(2,1)S(1)}, u32[]{:S(2)}, u32[]{:S(2)}) %collective-permute-start.17) | collective-permute-done | bytes 589856 | tf_op jit(solution)/shard_map/ppermute | solution.py:1116
  114.7 3.5 %collective-permute-start.21 = (bf16[192,1536]{1,0:T(8,128)(2,1)S(1)}, bf16[192,1536]{1,0:T(8,128)(2,1)S(1)}, u32[]{:S(2)}, u32[]{:S(2)}) collective-permute-start(bf16[192,1536]{1,0:T(8,128)(2,1)S(1)} %get-tuple-element.205.refs_3_), channel_id=1, source_target_pairs={{0,1},{3,2},{4,5},{7,6},{8,9},{11,10},{12,13},{15,14},{16,17},{19,... | collective-permute-start | bytes 1769480 | tf_op jit(solution)/shard_map/ppermute | solution.py:1126
  118.6 3.4 %up_grads.1 = (bf16[2,192,1536]{2,1,0:T(8,128)(2,1)S(1)}, bf16[2,192,1536]{2,1,0:T(8,128)(2,1)S(1)}, bf16[2,192,1536]{2,1,0:T(8,128)(2,1)S(1)}, bf16[2,192,1536]{2,1,0:T(8,128)(2,1)S(1)}, f32[8,128]{1,0:T(8,128)S(1)}) custom-call(s32[5]{0:T(128)S(1)} %copy-done.23, bf16[512,768]{1,0:T(8,128)(2,1)S(1)} %get-tuple-element.188.refs_1_, ...), custom_call_target="tpu_custom_call" | custom-call | flops 1 | bytes 1 | tf_op jit(solution)/shard_map/up_grads/pallas_call | solution.py:120
  122.1 5.0 %attend_back.2 = (bf16[512,384]{1,0:T(8,128)(2,1)S(1)}, f32[2,512,384]{2,1,0:T(8,128)S(1)}, bf16[2,512,384]{2,1,0:T(8,128)(2,1)S(1)}, f32[8,128]{1,0:T(8,128)S(1)}) custom-call(bf16[512,768]{1,0:T(8,128)(2,1)S(1)} %get-tuple-element.157.refs_0_, bf16[2,512,384]{2,1,0:T(8,128)(2,1)S(1)} %copy-done.32, bf16[2,512,384]{2,1,0:T(8,128)(2,1)S(1)} %copy-done.34, ...), custom_call_target="tpu_custom_call" | custom-call | flops 60000002048 | bytes 62914560 | tf_op jit(solution)/shard_map/attend_back/pallas_call | solution.py:120
  127.1 1.6 collective-permute-start.22
  130.7 4.4 %collective-permute-start.23 = (bf16[192,1536]{1,0:T(8,128)(2,1)S(1)}, bf16[192,1536]{1,0:T(8,128)(2,1)S(1)}, u32[]{:S(2)}, u32[]{:S(2)}) collective-permute-start(bf16[192,1536]{1,0:T(8,128)(2,1)S(1)} %get-tuple-element.214.refs_1_), channel_id=1, source_target_pairs={{0,1},{3,2},{4,5},{7,6},{8,9},{11,10},{12,13},{15,14},{16,17},{19,... | collective-permute-start | bytes 1769480 | tf_op jit(solution)/shard_map/ppermute | solution.py:1126
  138.5 5.0 %attend_back.3 = (bf16[512,384]{1,0:T(8,128)(2,1)S(1)}, f32[2,512,384]{2,1,0:T(8,128)S(1)}, bf16[2,528,384]{2,1,0:T(8,128)(2,1)S(1)}, f32[8,128]{1,0:T(8,128)S(1)}) custom-call(bf16[512,768]{1,0:T(8,128)(2,1)S(1)} %copy-done.30, bf16[2,528,384]{2,1,0:T(8,128)(2,1)S(1)} %get-tuple-element.163.refs_1_, ...), custom_call_target="tpu_custom_call" | custom-call | flops 60000002048 | bytes 62914560 | tf_op jit(solution)/shard_map/attend_back/pallas_call | solution.py:120
  143.5 2.4 collective-permute-done.23.refs_2_
  145.9 4.3 %collective-permute-done.24.refs_4_ = bf16[192,1536]{1,0:T(8,128)(2,1)S(1)} collective-permute-done((bf16[192,1536]{1,0:T(8,128)(2,1)S(1)}, bf16[192,1536]{1,0:T(8,128)(2,1)S(1)}, u32[]{:S(2)}, u32[]{:S(2)}) %collective-permute-start.24) | collective-permute-done | bytes 589856 | tf_op jit(solution)/shard_map/ppermute | solution.py:1116
  151.8 2.2 collective-permute-start.27
  154.7 1.6 collective-permute-start.33
  156.3 3.5 %lead_grads.1 = (bf16[2,512,384]{2,1,0:T(8,128)(2,1)S(1)}, bf16[2,192,2304]{2,1,0:T(8,128)(2,1)S(1)}, bf16[2,192,2304]{2,1,0:T(8,128)(2,1)S(1)}, f32[8,128]{1,0:T(8,128)S(1)}) custom-call(s32[5]{0:T(128)S(1)} %copy-done.23, bf16[512,384]{1,0:T(8,128)(2,1)S(1)} %get-tuple-element.162.refs_2_.refs_1_, bf16[512,384]{1,0:T(8,128)(2,1)S(1)} %get-tuple-element.167.refs_3_.refs_2_, ...), custom_call_target="tpu_custom_call" | custom-call | flops 1 | bytes 1 | tf_op jit(solution)/shard_map/lead_grads/pallas_call | solution.py:120
  159.8 3.6 %collective-permute-done.28.refs_4_ = bf16[192,1536]{1,0:T(8,128)(2,1)S(1)} collective-permute-done((bf16[192,1536]{1,0:T(8,128)(2,1)S(1)}, bf16[192,1536]{1,0:T(8,128)(2,1)S(1)}, u32[]{:S(2)}, u32[]{:S(2)}) %collective-permute-start.28) | collective-permute-done | bytes 589856 | tf_op jit(solution)/shard_map/ppermute | solution.py:1116
  165.1 3.7 %collective-permute-start.30 = (bf16[192,1536]{1,0:T(8,128)(2,1)S(1)}, bf16[192,1536]{1,0:T(8,128)(2,1)S(1)}, u32[]{:S(2)}, u32[]{:S(2)}) collective-permute-start(bf16[192,1536]{1,0:T(8,128)(2,1)S(1)} %get-tuple-element.230.refs_2_), channel_id=1, source_target_pairs={{0,1},{1,0},{2,3},{3,2},{4,5},{5,4},{6,7},{7,6},{8,9},{9,8},{10,11... | collective-permute-start | bytes 1769480 | tf_op jit(solution)/shard_map/ppermute | solution.py:1126
  170.7 1.6 collective-permute-start.31
  172.3 6.1 %first.1 = (f32[512,768]{1,0:T(8,128)}, bf16[400,768]{1,0:T(8,128)(2,1)S(1)}, bf16[400,768]{1,0:T(8,128)(2,1)S(1)}, f32[8,128]{1,0:T(8,128)S(1)}) custom-call(s32[5]{0:T(128)S(1)} %copy-done.23, f32[512,768]{1,0:T(8,128)S(1)} %get-tuple-element.234.refs_1_, bf16[512,768]{1,0:T(8,128)(2,1)S(1)} %copy-done.4, ...), custom_call_target="tpu_custom_call" | custom-call | flops 1 | bytes 1 | tf_op jit(solution)/shard_map/first/pallas_call | solution.py:120
  178.3 3.1 %collective-permute-done.31.refs_4_ = bf16[192,1536]{1,0:T(8,128)(2,1)S(1)} collective-permute-done((bf16[192,1536]{1,0:T(8,128)(2,1)S(1)}, bf16[192,1536]{1,0:T(8,128)(2,1)S(1)}, u32[]{:S(2)}, u32[]{:S(2)}) %collective-permute-start.31) | collective-permute-done | bytes 589856 | tf_op jit(solution)/shard_map/ppermute | solution.py:1116
  182.4 1.6 collective-permute-start.36
  184.0 2.1 collective-permute-start.34
  188.1 2.6 %settle.3 = (f32[768,768]{1,0:T(8,128)}, f32[8,128]{1,0:T(8,128)S(1)}) custom-call(s32[5]{0:T(128)S(1)} %copy-done.23, bf16[192,1536]{1,0:T(8,128)(2,1)S(1)} %get-tuple-element.223.refs_1_, bf16[192,1536]{1,0:T(8,128)(2,1)S(1)} %get-tuple-element.230.refs_2_, bf16[192,1536]{1,0:T(8,128)(2,1)S(1)} %collective-permute-done.27.refs_2_.refs_3_, ...), custom_call_target="tpu_custom_call" | custom-call | flops 1 | bytes 1 | tf_op jit(solution)/shard_map/settle/pallas_call | solution.py:120
  192.0 4.1 %collective-permute-done.34.refs_2_.refs_3_ = bf16[192,1536]{1,0:T(8,128)(2,1)S(1)} collective-permute-done((bf16[192,1536]{1,0:T(8,128)(2,1)S(1)}, bf16[192,1536]{1,0:T(8,128)(2,1)S(1)}, u32[]{:S(2)}, u32[]{:S(2)}) %collective-permute-start.34) | collective-permute-done | bytes 589856 | tf_op jit(solution)/shard_map/ppermute | solution.py:1126
  199.0 7.6 %collective-permute-start.38 = (bf16[192,768]{1,0:T(8,128)(2,1)S(1)}, bf16[192,768]{1,0:T(8,128)(2,1)S(1)}, u32[]{:S(2)}, u32[]{:S(2)}) collective-permute-start(bf16[192,768]{1,0:T(8,128)(2,1)S(1)} %get-tuple-element.251.refs_1_), channel_id=1, source_target_pairs={{0,1},{3,2},{4,5},{7,6},{8,9},{11,10},{12,13},{15,14},{16,17},{19,... | collective-permute-start | bytes 884744 | tf_op jit(solution)/shard_map/ppermute | solution.py:1126
  208.6 2.9 %collective-permute-done.38.refs_2_ = bf16[192,768]{1,0:T(8,128)(2,1)S(1)} collective-permute-done((bf16[192,768]{1,0:T(8,128)(2,1)S(1)}, bf16[192,768]{1,0:T(8,128)(2,1)S(1)}, u32[]{:S(2)}, u32[]{:S(2)}) %collective-permute-start.38) | collective-permute-done | bytes 294944 | tf_op jit(solution)/shard_map/ppermute | solution.py:1126
  212.1 1.6 collective-permute-start.40
  218.3 2.2 settle.4
  225.1 2.3 collective-permute-done.46.refs_4_.refs_3_
  228.6 9.6 %collective-permute-done.48.refs_4_ = bf16[192,768]{1,0:T(8,128)(2,1)S(1)} collective-permute-done((bf16[192,768]{1,0:T(8,128)(2,1)S(1)}, bf16[192,768]{1,0:T(8,128)(2,1)S(1)}, u32[]{:S(2)}, u32[]{:S(2)}) %collective-permute-start.48) | collective-permute-done | bytes 294944 | tf_op jit(solution)/shard_map/ppermute | solution.py:1126
  238.2 2.1 settle.5
  241.6 2.0 last_settle.1
  (174 shorter events, 53.8 us)
Async XLA Ops:
  3.1 24.2 %collective-permute-start.1 = (bf16[208,2304]{1,0:T(8,128)(2,1)S(1)}, bf16[208,2304]{1,0:T(8,128)(2,1)S(1)}, u32[]{:S(2)}, u32[]{:S(2)}) collective-permute-start(bf16[208,2304]{1,0:T(8,128)(2,1)S(1)} %get-tuple-element.150.refs_2_.refs_7_), channel_id=1, source_target_pairs={{0,8},{4,12},{8,0},{12,4},{16,24},{20,28},{24,16},{28,20},{1,9},{5... | collective-permute-start | bytes 2875400 | tf_op jit(solution)/shard_map/ppermute | solution.py:1116
  6.1 21.2 %collective-permute-start = (bf16[208,2304]{1,0:T(8,128)(2,1)S(1)}, bf16[208,2304]{1,0:T(8,128)(2,1)S(1)}, u32[]{:S(2)}, u32[]{:S(2)}) collective-permute-start(bf16[208,2304]{1,0:T(8,128)(2,1)S(1)} %get-tuple-element.150.refs_2_.refs_7_), channel_id=1, source_target_pairs={{0,4},{4,0},{8,12},{12,8},{16,20},{20,16},{24,28},{28,24},{1,5},{5... | collective-permute-start | bytes 2875400 | tf_op jit(solution)/shard_map/ppermute | solution.py:1116
  6.1 20.3 %collective-permute-start.2 = (bf16[512,768]{1,0:T(8,128)(2,1)}, bf16[512,768]{1,0:T(8,128)(2,1)}, u32[]{:S(2)}, u32[]{:S(2)}) collective-permute-start(bf16[512,768]{1,0:T(8,128)(2,1)} %refs_4_.3), channel_id=1, source_target_pairs={{0,16},{4,20},{8,24},{12,28},{16,0},{20,4},{24,8},{28,12},{1,17},{... | collective-permute-start | bytes 2359304 | tf_op jit(solution)/shard_map/ppermute | solution.py:1122
  12.9 16.4 %collective-permute-start.4 = (bf16[192,3840]{1,0:T(8,128)(2,1)S(1)}, bf16[192,3840]{1,0:T(8,128)(2,1)S(1)}, u32[]{:S(2)}, u32[]{:S(2)}) collective-permute-start(bf16[192,3840]{1,0:T(8,128)(2,1)S(1)} %get-tuple-element.153.refs_8_), channel_id=1, source_target_pairs={{0,4},{4,0},{8,12},{12,8},{16,20},{20,16},{24,28},{28,24},{1,5},{5... | collective-permute-start | bytes 4423688 | tf_op jit(solution)/shard_map/ppermute | solution.py:1116
  13.2 16.1 %collective-permute-start.5 = (bf16[768,768]{1,0:T(8,128)(2,1)S(1)}, bf16[768,768]{1,0:T(8,128)(2,1)S(1)}, u32[]{:S(2)}, u32[]{:S(2)}) collective-permute-start(bf16[768,768]{1,0:T(8,128)(2,1)S(1)} %get-tuple-element.154.refs_10_), channel_id=1, source_target_pairs={{0,4},{4,0},{8,12},{12,8},{16,20},{20,16},{24,28},{28,24},{1,5},{5... | collective-permute-start | bytes 3538952 | tf_op jit(solution)/shard_map/ppermute | solution.py:1116
  27.5 21.6 %collective-permute-start.7 = (bf16[272,1536]{1,0:T(8,128)(2,1)S(1)}, bf16[272,1536]{1,0:T(8,128)(2,1)}, u32[]{:S(2)}, u32[]{:S(2)}) collective-permute-start(bf16[272,1536]{1,0:T(8,128)(2,1)S(1)} %get-tuple-element.160), channel_id=1, source_target_pairs={{0,8},{4,12},{8,0},{12,4},{16,24},{20,28},{24,16},{28,20},{1,9},{5... | collective-permute-start | bytes 2506760 | tf_op jit(solution)/shard_map/ppermute | solution.py:1116
  33.7 19.7 %collective-permute-start.6 = (bf16[2,512,384]{2,1,0:T(8,128)(2,1)S(1)}, bf16[2,512,384]{2,1,0:T(8,128)(2,1)S(1)}, u32[]{:S(2)}, u32[]{:S(2)}) collective-permute-start(bf16[2,512,384]{2,1,0:T(8,128)(2,1)S(1)} %get-tuple-element.158.refs_1_), channel_id=1, source_target_pairs={{0,16},{4,20},{8,24},{12,28},{16,0},{20,4},{24,8},{28,12},{1,17},{... | collective-permute-start | bytes 2359304 | tf_op jit(solution)/shard_map/ppermute | solution.py:1122
  35.6 34.0 %collective-permute-start.10 = (bf16[192,2560]{1,0:T(8,128)(2,1)S(1)}, bf16[192,2560]{1,0:T(8,128)(2,1)S(1)}, u32[]{:S(2)}, u32[]{:S(2)}) collective-permute-start(bf16[192,2560]{1,0:T(8,128)(2,1)S(1)} %get-tuple-element.165), channel_id=1, source_target_pairs={{0,8},{4,12},{8,0},{12,4},{16,24},{20,28},{24,16},{28,20},{1,9},{5... | collective-permute-start | bytes 2949128 | tf_op jit(solution)/shard_map/ppermute | solution.py:1116
  49.0 25.3 %collective-permute-start.12 = (bf16[272,1536]{1,0:T(8,128)(2,1)}, bf16[272,1536]{1,0:T(8,128)(2,1)}, u32[]{:S(2)}, u32[]{:S(2)}) collective-permute-start(bf16[272,1536]{1,0:T(8,128)(2,1)} %hold.9.refs_5_.refs_14_), channel_id=1, source_target_pairs={{0,4},{4,0},{8,12},{12,8},{16,20},{20,16},{24,28},{28,24},{1,5},{5... | collective-permute-start | bytes 2506760 | tf_op jit(solution)/shard_map/ppermute | solution.py:1116
  49.0 21.3 %collective-permute-start.9 = (bf16[272,1536]{1,0:T(8,128)(2,1)}, bf16[272,1536]{1,0:T(8,128)(2,1)S(1)}, u32[]{:S(2)}, u32[]{:S(2)}) collective-permute-start(bf16[272,1536]{1,0:T(8,128)(2,1)} %hold.9.refs_5_.refs_14_), channel_id=1, source_target_pairs={{0,1},{1,0},{2,3},{3,2},{4,5},{5,4},{6,7},{7,6},{8,9},{9,8},{10,11... | collective-permute-start | bytes 2506760 | tf_op jit(solution)/shard_map/ppermute | solution.py:1126
  50.9 20.2 %collective-permute-start.8 = (bf16[2,528,384]{2,1,0:T(8,128)(2,1)S(1)}, bf16[2,528,384]{2,1,0:T(8,128)(2,1)S(1)}, u32[]{:S(2)}, u32[]{:S(2)}) collective-permute-start(bf16[2,528,384]{2,1,0:T(8,128)(2,1)S(1)} %get-tuple-element.163.refs_1_), channel_id=1, source_target_pairs={{0,16},{4,20},{8,24},{12,28},{16,0},{20,4},{24,8},{28,12},{1,17},{... | collective-permute-start | bytes 2433032 | tf_op jit(solution)/shard_map/ppermute | solution.py:1122
  69.5 4.8 %collective-permute-start.11 = (bf16[192,2560]{1,0:T(8,128)(2,1)S(1)}, bf16[192,2560]{1,0:T(8,128)(2,1)S(1)}, u32[]{:S(2)}, u32[]{:S(2)}) collective-permute-start(bf16[192,2560]{1,0:T(8,128)(2,1)S(1)} %hold.10.refs_1_.refs_12_), channel_id=1, source_target_pairs={{0,4},{4,0},{8,12},{12,8},{16,20},{20,16},{24,28},{28,24},{1,5},{5... | collective-permute-start | bytes 2949128 | tf_op jit(solution)/shard_map/ppermute | solution.py:1116
  70.4 4.0 %collective-permute-start.13 = (bf16[272,1536]{1,0:T(8,128)(2,1)S(1)}, bf16[272,1536]{1,0:T(8,128)(2,1)S(1)}, u32[]{:S(2)}, u32[]{:S(2)}) collective-permute-start(bf16[272,1536]{1,0:T(8,128)(2,1)S(1)} %hold.11.refs_5_.refs_15_), channel_id=1, source_target_pairs={{0,4},{4,0},{8,12},{12,8},{16,20},{20,16},{24,28},{28,24},{1,5},{5... | collective-permute-start | bytes 2506760 | tf_op jit(solution)/shard_map/ppermute | solution.py:1116
  84.9 3.8 %collective-permute-start.14 = (f32[8,512]{1,0:T(8,128)S(1)}, f32[8,512]{1,0:T(8,128)S(1)}, u32[]{:S(2)}, u32[]{:S(2)}) collective-permute-start(f32[8,512]{1,0:T(8,128)S(1)} %get-tuple-element.171.refs_2_.refs_8_), channel_id=1, source_target_pairs={{0,16},{4,20},{8,24},{12,28},{16,0},{20,4},{24,8},{28,12},{1,17},{... | collective-permute-start | bytes 49160 | tf_op jit(solution)/shard_map/ppermute | solution.py:1122
  93.0 2.9 %collective-permute-start.16 = (bf16[2,192,1536]{2,1,0:T(8,128)(2,1)S(1)}, bf16[2,192,1536]{2,1,0:T(8,128)(2,1)S(1)}, u32[]{:S(2)}, u32[]{:S(2)}) collective-permute-start(bf16[2,192,1536]{2,1,0:T(8,128)(2,1)S(1)} %get-tuple-element.182), channel_id=1, source_target_pairs={{0,4},{4,0},{8,12},{12,8},{16,20},{20,16},{24,28},{28,24},{1,5},{5... | collective-permute-start | bytes 3538952 | tf_op jit(solution)/shard_map/ppermute | solution.py:1116
  95.1 3.2 %collective-permute-start.15 = (bf16[2,192,1536]{2,1,0:T(8,128)(2,1)S(1)}, bf16[2,192,1536]{2,1,0:T(8,128)(2,1)S(1)}, u32[]{:S(2)}, u32[]{:S(2)}) collective-permute-start(bf16[2,192,1536]{2,1,0:T(8,128)(2,1)S(1)} %get-tuple-element.180), channel_id=1, source_target_pairs={{0,4},{4,0},{8,12},{12,8},{16,20},{20,16},{24,28},{28,24},{1,5},{5... | collective-permute-start | bytes 3538952 | tf_op jit(solution)/shard_map/ppermute | solution.py:1116
  96.7 15.4 %collective-permute-start.17 = (bf16[192,1536]{1,0:T(8,128)(2,1)S(1)}, bf16[192,1536]{1,0:T(8,128)(2,1)S(1)}, u32[]{:S(2)}, u32[]{:S(2)}) collective-permute-start(bf16[192,1536]{1,0:T(8,128)(2,1)S(1)} %get-tuple-element.193), channel_id=1, source_target_pairs={{0,8},{4,12},{8,0},{12,4},{16,24},{20,28},{24,16},{28,20},{1,9},{5... | collective-permute-start | bytes 1769480 | tf_op jit(solution)/shard_map/ppermute | solution.py:1116
  113.1 16.1 %collective-permute-start.20 = (bf16[192,1536]{1,0:T(8,128)(2,1)S(1)}, bf16[192,1536]{1,0:T(8,128)(2,1)S(1)}, u32[]{:S(2)}, u32[]{:S(2)}) collective-permute-start(bf16[192,1536]{1,0:T(8,128)(2,1)S(1)} %hold.12.refs_2_), channel_id=1, source_target_pairs={{0,8},{4,12},{8,0},{12,4},{16,24},{20,28},{24,16},{28,20},{1,9},{5... | collective-permute-start | bytes 1769480 | tf_op jit(solution)/shard_map/ppermute | solution.py:1116
  114.7 15.2 %collective-permute-start.21 = (bf16[192,1536]{1,0:T(8,128)(2,1)S(1)}, bf16[192,1536]{1,0:T(8,128)(2,1)S(1)}, u32[]{:S(2)}, u32[]{:S(2)}) collective-permute-start(bf16[192,1536]{1,0:T(8,128)(2,1)S(1)} %get-tuple-element.205.refs_3_), channel_id=1, source_target_pairs={{0,1},{3,2},{4,5},{7,6},{8,9},{11,10},{12,13},{15,14},{16,17},{19,... | collective-permute-start | bytes 1769480 | tf_op jit(solution)/shard_map/ppermute | solution.py:1126
  127.1 29.2 %collective-permute-start.22 = (bf16[2,512,384]{2,1,0:T(8,128)(2,1)S(1)}, bf16[2,512,384]{2,1,0:T(8,128)(2,1)S(1)}, u32[]{:S(2)}, u32[]{:S(2)}) collective-permute-start(bf16[2,512,384]{2,1,0:T(8,128)(2,1)S(1)} %get-tuple-element.212), channel_id=1, source_target_pairs={{0,16},{4,20},{8,24},{12,28},{16,0},{20,4},{24,8},{28,12},{1,17},{... | collective-permute-start | bytes 2359304 | tf_op jit(solution)/shard_map/ppermute | solution.py:1122
  128.7 9.0 %collective-permute-start.18 = (bf16[2,192,1536]{2,1,0:T(8,128)(2,1)S(1)}, bf16[2,192,1536]{2,1,0:T(8,128)(2,1)S(1)}, u32[]{:S(2)}, u32[]{:S(2)}) collective-permute-start(bf16[2,192,1536]{2,1,0:T(8,128)(2,1)S(1)} %get-tuple-element.201), channel_id=1, source_target_pairs={{0,4},{4,0},{8,12},{12,8},{16,20},{20,16},{24,28},{28,24},{1,5},{5... | collective-permute-start | bytes 3538952 | tf_op jit(solution)/shard_map/ppermute | solution.py:1116
  128.7 7.6 %collective-permute-start.19 = (bf16[2,192,1536]{2,1,0:T(8,128)(2,1)S(1)}, bf16[2,192,1536]{2,1,0:T(8,128)(2,1)S(1)}, u32[]{:S(2)}, u32[]{:S(2)}) collective-permute-start(bf16[2,192,1536]{2,1,0:T(8,128)(2,1)S(1)} %get-tuple-element.203), channel_id=1, source_target_pairs={{0,4},{4,0},{8,12},{12,8},{16,20},{20,16},{24,28},{28,24},{1,5},{5... | collective-permute-start | bytes 3538952 | tf_op jit(solution)/shard_map/ppermute | solution.py:1116
  130.7 15.2 %collective-permute-start.23 = (bf16[192,1536]{1,0:T(8,128)(2,1)S(1)}, bf16[192,1536]{1,0:T(8,128)(2,1)S(1)}, u32[]{:S(2)}, u32[]{:S(2)}) collective-permute-start(bf16[192,1536]{1,0:T(8,128)(2,1)S(1)} %get-tuple-element.214.refs_1_), channel_id=1, source_target_pairs={{0,1},{3,2},{4,5},{7,6},{8,9},{11,10},{12,13},{15,14},{16,17},{19,... | collective-permute-start | bytes 1769480 | tf_op jit(solution)/shard_map/ppermute | solution.py:1126
  135.1 10.8 %collective-permute-start.25 = (bf16[192,1536]{1,0:T(8,128)(2,1)S(1)}, bf16[192,1536]{1,0:T(8,128)(2,1)S(1)}, u32[]{:S(2)}, u32[]{:S(2)}) collective-permute-start(bf16[192,1536]{1,0:T(8,128)(2,1)S(1)} %get-tuple-element.217.refs_5_), channel_id=1, source_target_pairs={{1,2},{2,1},{5,6},{6,5},{9,10},{10,9},{13,14},{14,13},{17,18},{18,... | collective-permute-start | bytes 1769480 | tf_op jit(solution)/shard_map/ppermute | solution.py:1126
  137.1 13.1 %collective-permute-start.24 = (bf16[192,1536]{1,0:T(8,128)(2,1)S(1)}, bf16[192,1536]{1,0:T(8,128)(2,1)S(1)}, u32[]{:S(2)}, u32[]{:S(2)}) collective-permute-start(bf16[192,1536]{1,0:T(8,128)(2,1)S(1)} %get-tuple-element.216), channel_id=1, source_target_pairs={{0,8},{4,12},{8,0},{12,4},{16,24},{20,28},{24,16},{28,20},{1,9},{5... | collective-permute-start | bytes 1769480 | tf_op jit(solution)/shard_map/ppermute | solution.py:1116
  151.2 12.2 %collective-permute-start.28 = (bf16[192,1536]{1,0:T(8,128)(2,1)S(1)}, bf16[192,1536]{1,0:T(8,128)(2,1)S(1)}, u32[]{:S(2)}, u32[]{:S(2)}) collective-permute-start(bf16[192,1536]{1,0:T(8,128)(2,1)S(1)} %hold.13.refs_9_), channel_id=1, source_target_pairs={{0,8},{4,12},{8,0},{12,4},{16,24},{20,28},{24,16},{28,20},{1,9},{5... | collective-permute-start | bytes 1769480 | tf_op jit(solution)/shard_map/ppermute | solution.py:1116
  151.8 12.3 %collective-permute-start.27 = (bf16[192,1536]{1,0:T(8,128)(2,1)S(1)}, bf16[192,1536]{1,0:T(8,128)(2,1)S(1)}, u32[]{:S(2)}, u32[]{:S(2)}) collective-permute-start(bf16[192,1536]{1,0:T(8,128)(2,1)S(1)} %get-tuple-element.223.refs_1_), channel_id=1, source_target_pairs={{0,1},{1,0},{2,3},{3,2},{4,5},{5,4},{6,7},{7,6},{8,9},{9,8},{10,11... | collective-permute-start | bytes 1769480 | tf_op jit(solution)/shard_map/ppermute | solution.py:1126
  154.0 10.1 %collective-permute-start.29 = (bf16[192,1536]{1,0:T(8,128)(2,1)S(1)}, bf16[192,1536]{1,0:T(8,128)(2,1)S(1)}, u32[]{:S(2)}, u32[]{:S(2)}) collective-permute-start(bf16[192,1536]{1,0:T(8,128)(2,1)S(1)} %get-tuple-element.225.refs_5_), channel_id=1, source_target_pairs={{1,2},{2,1},{5,6},{6,5},{9,10},{10,9},{13,14},{14,13},{17,18},{18,... | collective-permute-start | bytes 1769480 | tf_op jit(solution)/shard_map/ppermute | solution.py:1126
  154.7 17.6 %collective-permute-start.33 = (bf16[2,528,384]{2,1,0:T(8,128)(2,1)S(1)}, bf16[2,528,384]{2,1,0:T(8,128)(2,1)S(1)}, u32[]{:S(2)}, u32[]{:S(2)}) collective-permute-start(bf16[2,528,384]{2,1,0:T(8,128)(2,1)S(1)} %get-tuple-element.236), channel_id=1, source_target_pairs={{0,16},{4,20},{8,24},{12,28},{16,0},{20,4},{24,8},{28,12},{1,17},{... | collective-permute-start | bytes 2433032 | tf_op jit(solution)/shard_map/ppermute | solution.py:1122
  159.8 9.9 %collective-permute-start.26 = (bf16[2,192,2304]{2,1,0:T(8,128)(2,1)S(1)}, bf16[2,192,2304]{2,1,0:T(8,128)(2,1)S(1)}, u32[]{:S(2)}, u32[]{:S(2)}) collective-permute-start(bf16[2,192,2304]{2,1,0:T(8,128)(2,1)S(1)} %get-tuple-element.221), channel_id=1, source_target_pairs={{0,4},{4,0},{8,12},{12,8},{16,20},{20,16},{24,28},{28,24},{1,5},{5... | collective-permute-start | bytes 5308424 | tf_op jit(solution)/shard_map/ppermute | solution.py:1116
  165.1 13.2 %collective-permute-start.30 = (bf16[192,1536]{1,0:T(8,128)(2,1)S(1)}, bf16[192,1536]{1,0:T(8,128)(2,1)S(1)}, u32[]{:S(2)}, u32[]{:S(2)}) collective-permute-start(bf16[192,1536]{1,0:T(8,128)(2,1)S(1)} %get-tuple-element.230.refs_2_), channel_id=1, source_target_pairs={{0,1},{1,0},{2,3},{3,2},{4,5},{5,4},{6,7},{7,6},{8,9},{9,8},{10,11... | collective-permute-start | bytes 1769480 | tf_op jit(solution)/shard_map/ppermute | solution.py:1126
  168.8 9.5 %collective-permute-start.32 = (bf16[192,1536]{1,0:T(8,128)(2,1)S(1)}, bf16[192,1536]{1,0:T(8,128)(2,1)S(1)}, u32[]{:S(2)}, u32[]{:S(2)}) collective-permute-start(bf16[192,1536]{1,0:T(8,128)(2,1)S(1)} %get-tuple-element.233.refs_5_), channel_id=1, source_target_pairs={{1,2},{2,1},{5,6},{6,5},{9,10},{10,9},{13,14},{14,13},{17,18},{18,... | collective-permute-start | bytes 1769480 | tf_op jit(solution)/shard_map/ppermute | solution.py:1126
  170.7 10.7 %collective-permute-start.31 = (bf16[192,1536]{1,0:T(8,128)(2,1)S(1)}, bf16[192,1536]{1,0:T(8,128)(2,1)S(1)}, u32[]{:S(2)}, u32[]{:S(2)}) collective-permute-start(bf16[192,1536]{1,0:T(8,128)(2,1)S(1)} %get-tuple-element.232), channel_id=1, source_target_pairs={{0,8},{4,12},{8,0},{12,4},{16,24},{20,28},{24,16},{28,20},{1,9},{5... | collective-permute-start | bytes 1769480 | tf_op jit(solution)/shard_map/ppermute | solution.py:1116
  178.3 8.5 %collective-permute-start.37 = (bf16[400,768]{1,0:T(8,128)(2,1)S(1)}, bf16[400,768]{1,0:T(8,128)(2,1)S(1)}, u32[]{:S(2)}, u32[]{:S(2)}) collective-permute-start(bf16[400,768]{1,0:T(8,128)(2,1)S(1)} %get-tuple-element.248), channel_id=1, source_target_pairs={{0,4},{4,0},{8,12},{12,8},{16,20},{20,16},{24,28},{28,24},{1,5},{5... | collective-permute-start | bytes 1843208 | tf_op jit(solution)/shard_map/ppermute | solution.py:1116
  182.4 9.6 %collective-permute-start.36 = (bf16[192,768]{1,0:T(8,128)(2,1)S(1)}, bf16[192,768]{1,0:T(8,128)(2,1)S(1)}, u32[]{:S(2)}, u32[]{:S(2)}) collective-permute-start(bf16[192,768]{1,0:T(8,128)(2,1)S(1)} %hold.14.refs_1_), channel_id=1, source_target_pairs={{0,8},{4,12},{8,0},{12,4},{16,24},{20,28},{24,16},{28,20},{1,9},{5... | collective-permute-start | bytes 884744 | tf_op jit(solution)/shard_map/ppermute | solution.py:1116
  184.0 12.1 %collective-permute-start.34 = (bf16[192,1536]{1,0:T(8,128)(2,1)S(1)}, bf16[192,1536]{1,0:T(8,128)(2,1)S(1)}, u32[]{:S(2)}, u32[]{:S(2)}) collective-permute-start(bf16[192,1536]{1,0:T(8,128)(2,1)S(1)} %get-tuple-element.244.refs_1_), channel_id=1, source_target_pairs={{0,1},{1,0},{2,3},{3,2},{4,5},{5,4},{6,7},{7,6},{8,9},{9,8},{10,11... | collective-permute-start | bytes 1769480 | tf_op jit(solution)/shard_map/ppermute | solution.py:1126
  186.1 10.0 %collective-permute-start.35 = (bf16[192,1536]{1,0:T(8,128)(2,1)S(1)}, bf16[192,1536]{1,0:T(8,128)(2,1)S(1)}, u32[]{:S(2)}, u32[]{:S(2)}) collective-permute-start(bf16[192,1536]{1,0:T(8,128)(2,1)S(1)} %get-tuple-element.245.refs_3_), channel_id=1, source_target_pairs={{1,2},{2,1},{5,6},{6,5},{9,10},{10,9},{13,14},{14,13},{17,18},{18,... | collective-permute-start | bytes 1769480 | tf_op jit(solution)/shard_map/ppermute | solution.py:1126
  187.5 19.1 %collective-permute-start.39 = (bf16[208,768]{1,0:T(8,128)(2,1)S(1)}, bf16[208,768]{1,0:T(8,128)(2,1)S(1)}, u32[]{:S(2)}, u32[]{:S(2)}) collective-permute-start(bf16[208,768]{1,0:T(8,128)(2,1)S(1)} %get-tuple-element.253), channel_id=1, source_target_pairs={{0,8},{4,12},{8,0},{12,4},{16,24},{20,28},{24,16},{28,20},{1,9},{5... | collective-permute-start | bytes 958472 | tf_op jit(solution)/shard_map/ppermute | solution.py:1116
  197.0 17.9 %collective-permute-start.41 = (bf16[192,1536]{1,0:T(8,128)(2,1)S(1)}, bf16[192,1536]{1,0:T(8,128)(2,1)S(1)}, u32[]{:S(2)}, u32[]{:S(2)}) collective-permute-start(bf16[192,1536]{1,0:T(8,128)(2,1)S(1)} %get-tuple-element.257.refs_1_), channel_id=1, source_target_pairs={{1,2},{2,1},{5,6},{6,5},{9,10},{10,9},{13,14},{14,13},{17,18},{18,... | collective-permute-start | bytes 1769480 | tf_op jit(solution)/shard_map/ppermute | solution.py:1126
  197.7 17.2 %collective-permute-start.43 = (bf16[192,1536]{1,0:T(8,128)(2,1)S(1)}, bf16[192,1536]{1,0:T(8,128)(2,1)S(1)}, u32[]{:S(2)}, u32[]{:S(2)}) collective-permute-start(bf16[192,1536]{1,0:T(8,128)(2,1)S(1)} %get-tuple-element.259.refs_2_), channel_id=1, source_target_pairs={{1,0},{2,3},{5,4},{6,7},{9,8},{10,11},{13,12},{14,15},{17,16},{18,... | collective-permute-start | bytes 1769480 | tf_op jit(solution)/shard_map/ppermute | solution.py:1126
  199.0 12.4 %collective-permute-start.38 = (bf16[192,768]{1,0:T(8,128)(2,1)S(1)}, bf16[192,768]{1,0:T(8,128)(2,1)S(1)}, u32[]{:S(2)}, u32[]{:S(2)}) collective-permute-start(bf16[192,768]{1,0:T(8,128)(2,1)S(1)} %get-tuple-element.251.refs_1_), channel_id=1, source_target_pairs={{0,1},{3,2},{4,5},{7,6},{8,9},{11,10},{12,13},{15,14},{16,17},{19,... | collective-permute-start | bytes 884744 | tf_op jit(solution)/shard_map/ppermute | solution.py:1126
  207.3 7.6 %collective-permute-start.42 = (bf16[208,768]{1,0:T(8,128)(2,1)S(1)}, bf16[208,768]{1,0:T(8,128)(2,1)S(1)}, u32[]{:S(2)}, u32[]{:S(2)}) collective-permute-start(bf16[208,768]{1,0:T(8,128)(2,1)S(1)} %get-tuple-element.258.refs_3_), channel_id=1, source_target_pairs={{0,1},{3,2},{4,5},{7,6},{8,9},{11,10},{12,13},{15,14},{16,17},{19,... | collective-permute-start | bytes 958472 | tf_op jit(solution)/shard_map/ppermute | solution.py:1126
  212.1 13.0 %collective-permute-start.40 = (bf16[512,768]{1,0:T(8,128)(2,1)S(1)}, bf16[512,768]{1,0:T(8,128)(2,1)S(1)}, u32[]{:S(2)}, u32[]{:S(2)}) collective-permute-start(bf16[512,768]{1,0:T(8,128)(2,1)S(1)} %hold.15.refs_5_.refs_0_), channel_id=1, source_target_pairs={{0,16},{4,20},{8,24},{12,28},{16,0},{20,4},{24,8},{28,12},{1,17},{... | collective-permute-start | bytes 2359304 | tf_op jit(solution)/shard_map/ppermute | solution.py:1122
  215.6 11.8 %collective-permute-start.46 = (bf16[192,1536]{1,0:T(8,128)(2,1)S(1)}, bf16[192,1536]{1,0:T(8,128)(2,1)S(1)}, u32[]{:S(2)}, u32[]{:S(2)}) collective-permute-start(bf16[192,1536]{1,0:T(8,128)(2,1)S(1)} %get-tuple-element.266.refs_1_), channel_id=1, source_target_pairs={{1,0},{2,3},{5,4},{6,7},{9,8},{10,11},{13,12},{14,15},{17,16},{18,... | collective-permute-start | bytes 1769480 | tf_op jit(solution)/shard_map/ppermute | solution.py:1126
  216.9 5.5 %collective-permute-start.44 = (bf16[208,768]{1,0:T(8,128)(2,1)S(1)}, bf16[208,768]{1,0:T(8,128)(2,1)S(1)}, u32[]{:S(2)}, u32[]{:S(2)}) collective-permute-start(bf16[208,768]{1,0:T(8,128)(2,1)S(1)} %get-tuple-element.260.refs_1_), channel_id=1, source_target_pairs={{1,2},{2,1},{5,6},{6,5},{9,10},{10,9},{13,14},{14,13},{17,18},{18,... | collective-permute-start | bytes 958472 | tf_op jit(solution)/shard_map/ppermute | solution.py:1126
  217.6 2.9 %collective-permute-start.45 = (bf16[192,768]{1,0:T(8,128)(2,1)S(1)}, bf16[192,768]{1,0:T(8,128)(2,1)S(1)}, u32[]{:S(2)}, u32[]{:S(2)}) collective-permute-start(bf16[192,768]{1,0:T(8,128)(2,1)S(1)} %get-tuple-element.261.refs_1_), channel_id=1, source_target_pairs={{1,2},{2,1},{5,6},{6,5},{9,10},{10,9},{13,14},{14,13},{17,18},{18,... | collective-permute-start | bytes 884744 | tf_op jit(solution)/shard_map/ppermute | solution.py:1126
  221.1 17.1 %collective-permute-start.48 = (bf16[192,768]{1,0:T(8,128)(2,1)S(1)}, bf16[192,768]{1,0:T(8,128)(2,1)S(1)}, u32[]{:S(2)}, u32[]{:S(2)}) collective-permute-start(bf16[192,768]{1,0:T(8,128)(2,1)S(1)} %get-tuple-element.270.refs_2_), channel_id=1, source_target_pairs={{1,0},{2,3},{5,4},{6,7},{9,8},{10,11},{13,12},{14,15},{17,16},{18,... | collective-permute-start | bytes 884744 | tf_op jit(solution)/shard_map/ppermute | solution.py:1126
  223.0 18.6 %collective-permute-start.47 = (bf16[208,768]{1,0:T(8,128)(2,1)S(1)}, bf16[208,768]{1,0:T(8,128)(2,1)S(1)}, u32[]{:S(2)}, u32[]{:S(2)}) collective-permute-start(bf16[208,768]{1,0:T(8,128)(2,1)S(1)} %get-tuple-element.269.refs_1_), channel_id=1, source_target_pairs={{1,0},{2,3},{5,4},{6,7},{9,8},{10,11},{13,12},{14,15},{17,16},{18,... | collective-permute-start | bytes 958472 | tf_op jit(solution)/shard_map/ppermute | solution.py:1126
  (36 other events, 323.5 us)
